TPU v7x, 32 devices: a whole 2x2x4 slice. The times are simulated.
32 devices in a mesh: rep: 2 (over x), dom: 16 (over z, y, core).
Axes of the slice: x: 2, y: 2, z: 4, core: 2. Of those that a mesh axis runs over, the one named last changes fastest.
Arguments:
- positions: float32 [3, 32768], P(None, ('rep', 'dom')), parts along dimension 1, may hold values from -6 to 6
- species: int32 [32768], P(('rep', 'dom')), parts along dimension 0, may hold values from 0 to 7
- live_bins: int32 [32], P(('rep', 'dom')), parts along dimension 0, may hold values from 16 to 64, as said below
- edge_nbr: int32 [1048576], P(('rep', 'dom')), parts along dimension 0, may hold values from 0 to 1791, as said below
- ghost_index: int32 [6, 4096], P(None, ('rep', 'dom')), parts along dimension 1, may hold values from 0 to 1023, as said below
- zeta_table: float32 [8], replicated, may hold values from 0.5 to 2
- energy_scale: float32 [8], replicated, may hold values from 0.5 to 2
- center_embed: float32 [64, 8], replicated, may hold values from -6 to 6
- nbr_embed: float32 [64], replicated, may hold values from -6 to 6
- radial_weight: float32 [64, 8], replicated, may hold values from -2 to 2
- latent_weight: float32 [64, 64], replicated, may hold values from -0.75 to 0.75
- env_weight: float32 [64, 64], replicated, may hold values from -0.75 to 0.75
- mix_weight: float32 [64, 128], replicated, may hold values from -0.5 to 0.5
- out_weight: float32 [64], replicated, may hold values from -0.75 to 0.75
Outputs:
- forces: float32 [3, 32768], P(None, ('rep', 'dom')), parts along dimension 1
There are 2 independent parts, one for each index of `rep`. A program takes and returns all parts, laid end to end along the dimension named above; an argument that names none is the same for every part. Nothing has to cross between parts.
Inputs may be any that keep to these rules, and one draw needn't show every extreme that they name: Bins below live_bins[d] of domain d are occupied and the others are empty; some domain has all 64 occupied. `edge_nbr`: values below 1024 name an atom of an occupied bin of the same domain; a value v of 1024 or more names ghost slot v - 1024, 128 slots a face in face order. Edges of even-numbered bins name the domain's own atoms only. `ghost_index`: every entry names an atom of an occupied bin of the sending domain.
All inputs are finite; a program needn't handle non-finite values.
Results may differ from a plain program's by a relative error of at most 0.0003.
Values sent between devices are 32-bit elements; how exact they have to be, the bound alone decides.
No kernel may reach another device: no remote copies, remote signals or barrier semaphores. Data moves between devices by JAX's collectives and lax.ppermute only.
A program may use at most 128 MiB of HBM per device.

v0:
```python
import functools
import math

import jax
import jax.numpy as jnp
from jax import lax
from jax.experimental import pallas as pl
from jax.experimental.pallas import tpu as pltpu
from jax.sharding import PartitionSpec as P

NBR = 32
BIN_ATOMS = 16
LANES = 128

FACES = ((1, 0, -1.0), (-1, 0, 1.0), (2, 1, -1.0), (-2, 1, 1.0), (8, 2, -1.0), (-8, 2, 1.0))
CUTOFF = 6.0
SOFTEN = 0.5
BOX_SHIFT = 3.0
F32 = jnp.float32
BF16 = jnp.bfloat16

SIN_TERMS = [(-1.0) ** i / math.factorial(2 * i + 1) for i in range(8)]
COS_TERMS = [(-1.0) ** i / math.factorial(2 * i) for i in range(8)]


def swap(block, size, step, flip):
    def partner(i):
        return (i + step if (i // step) % 2 == flip else i - step) % size

    return lax.ppermute(block, "dom", [(i, partner(i)) for i in range(size)])


def poly(terms, square):
    total = jnp.full_like(square, terms[-1])
    for term in terms[-2::-1]:
        total = total * square + term
    return total


def halves(x):
    top = x.astype(BF16)
    return top, (x - top.astype(F32)).astype(BF16)


def wide(x):
    top, rest = halves(x)
    return jnp.concatenate([top, top, rest], axis=1)


def stack(x, *more):
    top, rest = halves(x)
    return jnp.concatenate([top, rest, top, *more], axis=0)


def mm(left, right):
    return jnp.dot(left, right, preferred_element_type=F32)


def mm_nt(left, right):
    return lax.dot_general(left, right, (((1,), (1,)), ((), ())), preferred_element_type=F32)


def lookup(row, index):
    return jnp.take_along_axis(
        jnp.broadcast_to(row, index.shape), index, axis=1, mode="promise_in_bounds"
    )


def parity(step):
    return (lax.axis_index("dom") // step) % 2


def merged(step):
    return 2 * step == lax.axis_size("dom")


def face_slot(refs, a, flip, steps):
    place = 0
    for i, step in enumerate(steps):
        for f in range(1 if merged(step) else 2):
            if i == a and (f == flip or merged(step)):
                return refs[place - 1], 4 * flip if merged(step) else 0
            place += 1
    raise ValueError(a)


def prep_kernel(zeta_table, escale, live, pos, species, ghost_index, nbr, pack, *sends, steps):
    kinds = species[...]
    zeta = scale = jnp.zeros(kinds.shape, F32)
    for k in range(zeta_table.shape[0]):
        zeta = jnp.where(kinds == k, zeta_table[k], zeta)
        scale = jnp.where(kinds == k, escale[k], scale)
    width = kinds.shape[1]
    tiles = width // LANES
    live_row = jnp.full((1, LANES), live[0].astype(F32))
    for t in range(tiles):
        lane = slice(t * LANES, (t + 1) * LANES)
        parts = [pos[:, lane], zeta[:, lane], kinds[:, lane].astype(F32), live_row]
        pack[8 * t : 8 * t + 6, :] = jnp.concatenate(parts, axis=0)
        pack[8 * t + 6 : 8 * t + 7, :] = jnp.zeros((1, LANES), F32)
        pack[8 * t + 7 : 8 * t + 8, :] = scale[:, lane]
    pack[8 * tiles :, :] = nbr[...].astype(F32)
    index = ghost_index[...]
    index = jnp.concatenate([index, index[:2]], axis=0)
    low, high = index & (LANES - 1), index >> 7
    got = []
    for d in range(4):
        value = jnp.zeros(index.shape, F32)
        for t in range(tiles):
            row = pack[8 * t + d : 8 * t + d + 1, :]
            value = jnp.where(high == t, lookup(row, low), value)
        got.append(value)
    for a, step in enumerate(steps):
        par = parity(step)
        for flip in range(2):
            ahead = par == flip
            for d in range(4):
                first, second = got[d][2 * a : 2 * a + 1], got[d][2 * a + 1 : 2 * a + 2]
                if d == a:
                    first, second = first - BOX_SHIFT, second + BOX_SHIFT
                part = jnp.where(ahead, first, second)
                if a == 0 and flip == 0:
                    pack[8 * d + 6 : 8 * d + 7, :] = part
                else:
                    ref, row = face_slot(sends, a, flip, steps)
                    ref[row + d : row + d + 1, :] = part


def weights_kernel(pack, center_t, nbr_row, radial_t, latent, env, mix, out_row, *outs):
    pack_o, out_wide_o, out_row2_o = outs[:3]
    pack_o[...] = pack[...]
    chan = latent.shape[0]
    kinds_total = center_t.shape[0]
    norm = NBR ** (-0.5)
    nb = radial_t.shape[0]
    first = jnp.concatenate(
        [radial_t[...], nbr_row[...], jnp.zeros((LANES - nb - 1, chan), F32)], axis=0
    ).T
    centers = jnp.concatenate([center_t[...], jnp.zeros((LANES - kinds_total, chan), F32)], axis=0).T
    top, rest = halves(0.5 * centers[:, :8])
    w1 = jnp.concatenate([wide(0.5 * first[:, :16]), top, rest], axis=1)
    w2 = wide(0.5 * latent[...])
    mix_a = mix[:, :chan]
    mix_b = mix[:, chan:]
    row = out_row[...]
    w3 = wide(jnp.concatenate([0.5 * mix_a, row, jnp.zeros((15, chan), F32)], axis=0))
    both = (0.5 * norm) * mm(wide(mix_b), stack(env[...]))
    out_col = jnp.broadcast_to(row, (LANES, chan)).T
    out_wide_o[...] = jnp.concatenate([out_col, out_col], axis=1)
    _, orest = halves(out_col)
    lane16 = lax.broadcasted_iota(jnp.int32, (chan, 16), 1)
    extra = jnp.where(lane16 == 0, out_col[:, :16], 0.0).astype(BF16)
    extra = extra + jnp.where(lane16 == 1, orest[:, :16].astype(F32), 0.0).astype(BF16)
    w5 = jnp.concatenate([wide(mix_a.T * (0.5 * row)), extra], axis=1)
    out_row2_o[...] = jnp.concatenate([row, row], axis=1)

    def doubled(x):
        top, rest = halves(jnp.concatenate([jnp.concatenate([x, x], axis=0)] * 2, axis=1))
        return jnp.concatenate([top, top, rest], axis=0)

    w4 = doubled(both.T)
    w6 = doubled(out_col[:, :chan] * both)
    w7 = wide(0.5 * latent[...].T)
    last = jnp.concatenate([0.5 * radial_t[...], jnp.zeros((16 - nb, chan), F32)], axis=0)
    top, rest = halves(jnp.concatenate([last, last], axis=1))
    w8 = jnp.concatenate([top, rest], axis=0)
    for ref, value in zip(outs[3:], (w1, w2, w3, w4, w5, w6, w7, w8)):
        ref[...] = value


def edge_kernel(
    live,
    pack,
    mate,
    out_s,
    row2,
    *refs,
    steps,
    batch,
    basis_count,
    lag,
):
    nfaces = 2 * len(steps)
    nsends = sum(1 if merged(step) else 2 for step in steps) - 1
    ghosts = refs[:nsends]
    weights = refs[nsends : nsends + 8]
    own_out, mate_out = refs[nsends + 8 : nsends + 10]
    ghost_out = refs[nsends + 10 : 2 * nsends + 10]
    (
        table,
        index_s,
        basis_s,
        kinds_s,
        geo_s,
        red_s,
        outf_s,
        db_s,
        acc_s,
        own_s,
        df1_s,
        df2_s,
        f2_s,
        ua_s,
        ub_s,
        sel_s,
    ) = refs[2 * nsends + 10 :]
    chan = out_s.shape[0]
    nb = basis_count
    own_tiles = pack.shape[0] // (8 + NBR)
    tiles = own_tiles + nfaces
    group = LANES // BIN_ATOMS
    wide_row = 2 * LANES

    for t in range(own_tiles):
        table[0, t] = pack[8 * t : 8 * t + 8, :]
        table[1, t] = mate[8 * t : 8 * t + 8, :]
    for a, step in enumerate(steps):
        par = parity(step)
        for flip in range(2):
            tile = own_tiles + 2 * a + jnp.where(par == flip, 1, 0)
            for d in range(4):
                if a == 0 and flip == 0:
                    row = mate[8 * d + 6 : 8 * d + 7, :]
                else:
                    ref, first = face_slot(ghosts, a, flip, steps)
                    row = ref[first + d : first + d + 1, :]
                table[0, tile, d : d + 1, :] = row
    acc_s[...] = jnp.zeros(acc_s.shape, F32)
    own_s[...] = jnp.zeros(own_s.shape, F32)

    w1, w2, w3, w4, w5, w6, w7, w8 = [ref[...] for ref in weights]
    out_row2 = row2[...]
    sub16 = lax.broadcasted_iota(jnp.int32, (16, LANES), 0)
    sub16w = lax.broadcasted_iota(jnp.int32, (16, wide_row), 0)
    ones = jnp.where(sub16w < 2, 1.0, 0.0).astype(BF16)
    from_lane = lax.broadcasted_iota(jnp.int32, (LANES, LANES), 0)
    to_lane = lax.broadcasted_iota(jnp.int32, (LANES, LANES), 1)
    per_row = LANES // NBR
    sel_s[...] = jnp.where(from_lane // NBR == to_lane % per_row, 1.0, 0.0).astype(BF16)
    sub8 = lax.broadcasted_iota(jnp.int32, (8, LANES), 0)
    lane8 = lax.broadcasted_iota(jnp.int32, (8, LANES), 1)
    masks = [jnp.where(sub8 == h * per_row + lane8 // NBR, 1.0, 0.0) for h in range(2)]
    zero8 = jnp.zeros((8, LANES), F32)
    lower = lax.broadcasted_iota(jnp.int32, (NBR, LANES), 1) < chan

    mine = live[0]
    theirs = jnp.max(mate[5:6, :]).astype(jnp.int32)

    def counts(bins):
        even = ((bins + 1) // 2 + group - 1) // group
        odd = (bins // 2 + group - 1) // group
        return even, odd

    my_even, my_odd = counts(mine)
    their_even, their_odd = counts(theirs)
    excess = my_even + my_odd - their_even - their_odd
    give = jnp.minimum(jnp.maximum(excess, 0) // 2, my_even)
    take = jnp.minimum(jnp.maximum(-excess, 0) // 2, their_even)
    keep_even = my_even - give

    def slope2(u, f):
        return u + f * (2.0 - u)

    def block(i, carry):
        is_mate = i >= keep_even + my_odd
        is_odd = jnp.logical_and(i >= keep_even, jnp.logical_not(is_mate))
        which = jnp.where(is_mate, 1, 0)
        odd = jnp.where(is_odd, 1, 0)
        kb = jnp.where(
            is_mate, their_even - take + i - keep_even - my_odd, jnp.where(is_odd, i - keep_even, i)
        )
        bins = jnp.where(is_mate, theirs, mine)
        row0 = pl.multiple_of(64 * kb, 64)

        @pl.when(is_mate)
        def _():
            for part in range(4):
                got = mate[pl.ds(8 * own_tiles + row0 + part, 8, stride=8), :]
                index_s[8 * part : 8 * part + 8, :] = got

        @pl.when(jnp.logical_not(is_mate))
        def _():
            for part in range(4):
                start = 8 * own_tiles + row0 + 4 * odd + part
                index_s[8 * part : 8 * part + 8, :] = pack[pl.ds(start, 8, stride=8), :]

        index = index_s[...].astype(jnp.int32)
        low, high = index & (LANES - 1), index >> 7

        local = 2 * sub8 + odd
        bin_of = 16 * kb + local
        upper = sub8 < 4
        here = []
        for d in (0, 1, 2, 4, 7):
            source = jnp.where(
                upper,
                jnp.broadcast_to(table[which, 2 * kb, d : d + 1, :], (8, LANES)),
                jnp.broadcast_to(table[which, 2 * kb + 1, d : d + 1, :], (8, LANES)),
            )
            found = []
            for part in range(4):
                pick = (local % group) * BIN_ATOMS + part * per_row + lane8 // NBR
                found.append(jnp.take_along_axis(source, pick, axis=1, mode="promise_in_bounds"))
            here.append(jnp.concatenate(found, axis=0))
        kinds = here[3]
        kinds_s[...] = kinds
        occupied = jnp.concatenate([jnp.where(bin_of < bins, 1.0, 0.0)] * 4, axis=0)

        got = []
        for d in range(4):
            value = jnp.zeros((NBR, LANES), F32)
            for t in range(tiles):
                value = jnp.where(high == t, lookup(table[which, t, d : d + 1, :], low), value)
            got.append(value)
        disp = [got[d] - here[d] for d in range(3)]
        square = disp[0] * disp[0] + disp[1] * disp[1] + disp[2] * disp[2]
        dist = jnp.sqrt(square + SOFTEN * SOFTEN)
        inv_dist = 1.0 / dist
        unit = [disp[d] * inv_dist for d in range(3)]
        x = jnp.minimum(dist * (1.0 / CUTOFF), 1.0)
        inv_x = 1.0 / x
        gap = 1.0 - x * x
        envelope = gap * gap
        t = math.pi * (x - 0.5)
        tt = t * t
        s1 = poly(COS_TERMS, tt)
        c1 = -(t * poly(SIN_TERMS, tt))
        sins, coss = [s1], [c1]
        for k in range(2, nb + 1):
            p, q = k // 2 - 1, k - k // 2 - 1
            sins.append(sins[p] * coss[q] + coss[p] * sins[q])
            coss.append(coss[p] * coss[q] - sins[p] * sins[q])
        scale = envelope * inv_x
        for k in range(nb):
            basis_s[pl.ds(k, NBR, stride=16), :] = sins[k] * scale
        basis_s[pl.ds(nb, NBR, stride=16), :] = got[3]
        for k in range(nb + 1, 16):
            basis_s[pl.ds(k, NBR, stride=16), :] = jnp.zeros((NBR, LANES), F32)
        for d in range(3):
            for q, value in ((d, unit[d]), (6 + d, unit[d] * envelope)):
                top = value.astype(BF16).astype(F32)
                geo_s[q] = top
                geo_s[q + 3] = value - top

        def fold8(v):
            return sum(v[8 * j : 8 * j + 8] for j in range(1, chan // 8)) + v[:8]

        def parted(x):
            top = x.astype(BF16).astype(F32)
            return top, x - top

        def terms(top, rest):
            rows = jnp.concatenate([top[:24], top[:24], rest[:24], zero8], axis=0)
            return rows.T[:chan].astype(BF16)

        def centre_sum(both_parts, t):
            found = mm_nt(ub_s[t], both_parts)
            return found[:NBR] + jnp.where(lower, found[NBR:], 0.0)

        def spread_rows(sums, weight):
            top, rest = halves(jnp.concatenate(sums, axis=0))
            out = mm(jnp.concatenate([top, rest, top], axis=1), weight)
            return [out[NBR * i : NBR * i + NBR] for i in range(len(sums))]

        def pieces(q, r):
            return [geo_s[q + d, r : r + 1, :] * masks[r % 2] for d in range(3)]

        def cells(t):
            return [(2 * t + h, h, slice(h * LANES, (h + 1) * LANES)) for h in range(2)]

        z1, z2, z3, direct, sums, lefts, got5, v3, d1 = ({} for _ in range(9))

        def stage_basis(ts):
            for t in ts:
                cols = []
                for r, h, cell in cells(t):
                    hit = sub8.astype(F32) == kinds_s[r : r + 1, :]
                    onehot = jnp.where(hit, 1.0, 0.0)
                    onehot = jnp.concatenate([onehot, onehot], axis=0).astype(BF16)
                    cols.append(stack(basis_s[r * 16 : r * 16 + 16, :], onehot))
                z1[t] = mm(w1, jnp.concatenate(cols, axis=1))

        def stage_units(ts):
            for t in ts:
                for r, h, cell in cells(t):
                    a, b = pieces(0, r), pieces(3, r)
                    ua = jnp.concatenate([*a, *b, *a, zero8], axis=0)
                    ua_s[t, :, cell] = ua.astype(BF16)
                    a, b = pieces(6, r), pieces(9, r)
                    ub = jnp.concatenate([*a, zero8, *b, zero8], axis=0)
                    ub_s[t, :, cell] = ub.astype(BF16)

        def stage_first(ts):
            for t in ts:
                u = 1.0 + jnp.tanh(z1[t])
                f = z1[t] * u
                df1_s[t] = slope2(u, f)
                z2[t] = mm(w2, stack(f))

        def stage_second(ts):
            for t in ts:
                u = 1.0 + jnp.tanh(z2[t])
                f = z2[t] * u
                df2_s[t] = slope2(u, f)
                top, rest = halves(f)
                both_parts = jnp.concatenate([top, rest], axis=0)
                f2_s[t] = both_parts
                sums[t] = centre_sum(both_parts, t)
                direct[t] = mm(w3, jnp.concatenate([top, rest, top], axis=0))

        def stage_env(ts):
            for t, g in zip(ts, spread_rows([sums[t] for t in ts], w4)):
                lefts[t] = terms(*parted(g))
                top, rest = halves(g * out_row2)
                rest = jnp.where(lower, rest, 0.0)[:, :80]
                lefts[t, 1] = jnp.concatenate([w5, jnp.concatenate([top, rest], axis=1)], axis=0)

        def stage_mix(ts):
            for t in ts:
                z3[t] = mm(lefts[t], ua_s[t])

        def stage_third(ts):
            for t in ts:
                for r, h, cell in cells(t):
                    outf_s[r : r + 1, :] = direct[t][chan : chan + 1, cell]
                z = direct[t][:chan] + z3[t]
                u = 1.0 + jnp.tanh(z)
                f = z * u
                v = slope2(u, f)
                folded = fold8(f * out_s[...])
                for r, h, cell in cells(t):
                    red_s[6, 8 * r : 8 * r + 8, :] = folded[:, cell]
                top, rest = halves(v)
                sums[t] = centre_sum(jnp.concatenate([top, rest], axis=0), t)
                got5[t] = mm(lefts[t, 1], jnp.concatenate([top, rest, top, ones], axis=0))

        def stage_denv(ts):
            for t, g in zip(ts, spread_rows([sums[t] for t in ts], w6)):
                top, rest = parted(g)
                lefts[t] = terms(top, rest)
                lefts[t, 1] = jnp.concatenate([top, rest], axis=0).astype(BF16)
                for r, h, cell in cells(t):
                    for d in range(3):
                        part = got5[t][chan + 8 * d : chan + 8 * d + 8, cell]
                        red_s[d, 8 * r : 8 * r + 8, :] = part * masks[h]

        def stage_back(ts):
            for t in ts:
                v3[t] = mm(lefts[t], ua_s[t])

        def stage_slope2(ts):
            for t in ts:
                v = got5[t][:chan] + v3[t]
                d1[t] = mm(w7, stack(v * df2_s[t]))

        def stage_pull(ts):
            for t in ts:
                pulled = mm(lefts[t, 1], f2_s[t])
                for r, h, cell in cells(t):
                    for d in range(3):
                        part = pulled[8 * d : 8 * d + 8, cell] + pulled[NBR + 8 * d : NBR + 8 * d + 8, cell]
                        red_s[3 + d, 8 * r : 8 * r + 8, :] = part * masks[h]

        def stage_slope1(ts):
            for t in ts:
                top, rest = halves(d1[t] * df1_s[t])
                v = mm(w8, jnp.concatenate([top, rest], axis=0))
                v = v[:8] + v[16:24]
                for r, h, cell in cells(t):
                    db_s[8 * r : 8 * r + 8, :] = v[:, cell]

        stages = [
            stage_basis,
            stage_units,
            stage_first,
            stage_second,
            stage_env,
            stage_mix,
            stage_third,
            stage_denv,
            stage_back,
            stage_slope2,
            stage_pull,
            stage_slope1,
        ]
        groups = [range(t0, t0 + batch) for t0 in range(0, NBR // 2, batch)]
        for turn in range(len(stages) + (len(groups) - 1) * lag):
            for i, ts in enumerate(groups):
                if 0 <= turn - i * lag < len(stages):
                    stages[turn - i * lag](ts)

        def collect(ref, q):
            total = ref[q, pl.ds(0, NBR, stride=8), :]
            for k in range(1, 8):
                total = total + ref[q, pl.ds(k, NBR, stride=8), :]
            return total

        pulls = [collect(red_s, 3 + d) for d in range(3)]
        d_unit = [envelope * (collect(red_s, d) + pulls[d]) for d in range(3)]
        d_env = collect(red_s, 6) + outf_s[...]
        for d in range(3):
            d_env = d_env + unit[d] * pulls[d]
        along = jnp.zeros((NBR, LANES), F32)
        level = jnp.zeros((NBR, LANES), F32)
        for k in range(nb):
            g = db_s[pl.ds(k, NBR, stride=8), :]
            ratio = sins[k] * inv_x
            level = level + g * ratio
            along = along + g * ((k + 1) * math.pi * coss[k] - ratio)
        d_env = d_env + envelope * level
        d_x = envelope * envelope * inv_x * along - 4.0 * x * gap * d_env
        radial = d_x * (1.0 / CUTOFF)
        for d in range(3):
            radial = radial - d_unit[d] * unit[d] * inv_dist
        lefts = []
        for d in range(3):
            g = jnp.where(occupied > 0.0, (d_unit[d] * inv_dist + radial * unit[d]) * here[4], 0.0)
            top = g.astype(BF16).astype(F32)
            geo_s[2 * d] = top
            geo_s[2 * d + 1] = g - top
            lefts += [top, g - top]
        sums = mm(jnp.concatenate(lefts, axis=0).astype(BF16), sel_s[...])
        own_rows = []
        for d in range(3):
            total = jnp.zeros((8, LANES), F32)
            for part in range(4):
                row = 64 * d + 8 * part
                value = sums[row : row + 8] + sums[row + NBR : row + NBR + 8]
                total = total + jnp.where((lane8 % BIN_ATOMS) // per_row == part, value, 0.0)
            total = jnp.where(lane8 // BIN_ATOMS == local % group, total, 0.0)
            for h in range(2):
                own_rows.append(jnp.sum(jnp.where(upper == (h == 0), total, 0.0), axis=0, keepdims=True))
        for d in range(3):
            for h in range(2):
                own_s[which, d, pl.ds(2 * kb + h, 1), :] += own_rows[2 * d + h]

        lefts, rights = [], []
        for n in range(NBR):
            lows, highs = low[n : n + 1], high[n : n + 1]
            rights.append(jnp.where(from_lane == lows, 1.0, 0.0).astype(BF16))
            hit = sub16 == highs
            rows = [jnp.where(hit, geo_s[q, n : n + 1, :], 0.0) for q in range(6)]
            lefts.append(jnp.concatenate(rows, axis=0).astype(BF16))
        acc_s[which] += mm_nt(jnp.concatenate(lefts, axis=1), jnp.concatenate(rights, axis=1))
        return carry

    lax.fori_loop(0, keep_even + my_odd + take, block, 0)

    for d in range(3):
        for which in range(2):
            a = acc_s[which, 32 * d : 32 * d + 16, :] + acc_s[which, 32 * d + 16 : 32 * d + 32, :]
            a = own_s[which, d] - a
            for t in range(own_tiles):
                if which:
                    mate_out[4 * t + d : 4 * t + d + 1, :] = a[t : t + 1]
                else:
                    own_out[d : d + 1, t * LANES : (t + 1) * LANES] = a[t : t + 1]
            if which == 0:
                outf_s[0:16, :] = a
                for c, step in enumerate(steps):
                    par = parity(step)
                    for flip in range(2):
                        row = outf_s[pl.ds(own_tiles + 2 * c + jnp.where(par == flip, 1, 0), 1), :]
                        if c == 0 and flip == 0:
                            mate_out[4 * d + 3 : 4 * d + 4, :] = row
                        else:
                            ref, first = face_slot(ghost_out, c, flip, steps)
                            ref[first + d : first + d + 1, :] = row


def fold_kernel(own, back, ghost_index, *refs, steps):
    returned, out = refs[:-1], refs[-1]
    tiles = own.shape[1] // LANES
    lefts, rights = [], []
    for a, step in enumerate(steps):
        par = parity(step)
        for flip in range(2):
            index = ghost_index[pl.ds(2 * a + jnp.where(par == flip, 0, 1), 1), :]
            low, high = index & (LANES - 1), index >> 7
            hit = lax.broadcasted_iota(jnp.int32, (LANES, LANES), 0) == low
            rights.append(jnp.where(hit, 1.0, 0.0).astype(BF16))
            tile_hit = lax.broadcasted_iota(jnp.int32, (16, LANES), 0) == high
            rows = []
            for d in range(3):
                if a == 0 and flip == 0:
                    value = back[4 * d + 3 : 4 * d + 4, :]
                else:
                    ref, first = face_slot(returned, a, flip, steps)
                    value = ref[first + d : first + d + 1, :]
                rows.extend(halves(jnp.where(tile_hit, value, 0.0)))
            lefts.append(jnp.concatenate(rows, axis=0))
    total = mm_nt(jnp.concatenate(lefts, axis=1), jnp.concatenate(rights, axis=1))
    for d in range(3):
        a = total[32 * d : 32 * d + 16] + total[32 * d + 16 : 32 * d + 32]
        for t in range(tiles):
            lane = slice(t * LANES, (t + 1) * LANES)
            out[d : d + 1, lane] = own[d : d + 1, lane] + back[4 * t + d : 4 * t + d + 1, :] + a[t : t + 1]


VM = functools.partial(pl.BlockSpec, memory_space=pltpu.VMEM)
SM = functools.partial(pl.BlockSpec, memory_space=pltpu.SMEM)
SMALL = pltpu.CompilerParams(vmem_limit_bytes=4 * 1024 * 1024)


def shards(
    positions,
    species,
    live_bins,
    edge_nbr,
    ghost_index,
    zeta_table,
    energy_scale,
    center_embed,
    nbr_embed,
    radial_weight,
    latent_weight,
    env_weight,
    mix_weight,
    out_weight,
):
    size = lax.axis_size("dom")
    atoms = species.shape[0]
    chan = latent_weight.shape[0]
    ghosts = ghost_index.shape[1]
    steps = tuple(o for o, _, s in FACES if s < 0)
    shape = jax.ShapeDtypeStruct

    nbr = edge_nbr.reshape(atoms * NBR // LANES, LANES)
    tiles = atoms // LANES
    swaps = [(step, flip) for step in steps for flip in range(1 if 2 * step == size else 2)]
    buffers = [shape((8 if 2 * step == size else 4, ghosts), F32) for step, _ in swaps[1:]]

    def exchange(parts):
        return [swap(part, size, step, flip) for part, (step, flip) in zip(parts, swaps)]

    pack, *sends = pl.pallas_call(
        functools.partial(prep_kernel, steps=steps),
        out_shape=[shape((8 * tiles + nbr.shape[0], LANES), F32)] + buffers,
        in_specs=[SM(), SM(), SM()] + [VM()] * 4,
        out_specs=[VM()] * (1 + len(buffers)),
        name="prep",
    )(zeta_table, energy_scale, live_bins, positions, species.reshape(1, atoms), ghost_index, nbr)
    mate, *arrived = exchange([pack, *sends])

    heights = [(chan, 64), (chan, 3 * chan), (chan + 16, 3 * chan), (6 * chan, LANES)]
    heights += [(chan, 3 * chan + 16), (6 * chan, LANES), (chan, 3 * chan), (32, LANES)]
    pack_here, out_wide, out_row2, *weights = pl.pallas_call(
        weights_kernel,
        out_shape=[shape(pack.shape, F32), shape((chan, 2 * LANES), F32), shape((1, 2 * chan), F32)]
        + [shape(h, BF16) for h in heights],
        in_specs=[VM()] * 8,
        out_specs=[VM()] * (3 + len(heights)),
        compiler_params=SMALL,
        name="weights",
    )(
        pack,
        center_embed.T,
        nbr_embed.reshape(1, chan),
        radial_weight.T,
        latent_weight,
        env_weight,
        mix_weight,
        out_weight.reshape(1, chan),
    )

    pairs = NBR // 2
    big = pltpu.VMEM((pairs, chan, 2 * LANES), F32)
    own, mate_part, *parts = pl.pallas_call(
        functools.partial(edge_kernel, steps=steps, batch=8, lag=1, basis_count=radial_weight.shape[1]),
        out_shape=[shape((3, atoms), F32), shape((4 * tiles, LANES), F32)] + buffers,
        in_specs=[SM()] + [VM()] * (4 + len(buffers) + len(weights)),
        out_specs=[VM()] * (2 + len(buffers)),
        scratch_shapes=[
            pltpu.VMEM((2, 16, 8, LANES), F32),
            pltpu.VMEM((NBR, LANES), F32),
            pltpu.VMEM((NBR * 16, LANES), F32),
            pltpu.VMEM((NBR, LANES), F32),
            pltpu.VMEM((12, NBR, LANES), F32),
            pltpu.VMEM((7, NBR * 8, LANES), F32),
            pltpu.VMEM((NBR, LANES), F32),
            pltpu.VMEM((NBR * 8, LANES), F32),
            pltpu.VMEM((2, 96, LANES), F32),
            pltpu.VMEM((2, 3, 16, LANES), F32),
            big,
            big,
            pltpu.VMEM((pairs, 2 * chan, 2 * LANES), BF16),
            pltpu.VMEM((pairs, 80, 2 * LANES), BF16),
            pltpu.VMEM((pairs, 2 * NBR, 2 * LANES), BF16),
            pltpu.VMEM((LANES, LANES), BF16),
        ],
        compiler_params=pltpu.CompilerParams(vmem_limit_bytes=24 * 1024 * 1024),
        name="edges",
    )(live_bins, pack_here, mate, out_wide, out_row2, *arrived, *weights)
    back, *returned = exchange([mate_part, *parts])
    return pl.pallas_call(
        functools.partial(fold_kernel, steps=steps),
        out_shape=shape((3, atoms), F32),
        in_specs=[VM()] * (3 + len(buffers)),
        out_specs=VM(),
        compiler_params=SMALL,
        name="fold",
    )(own, back, ghost_index, *returned)


def solution(mesh):
    in_specs = (
        P(None, ("rep", "dom")),
        P(("rep", "dom")),
        P(("rep", "dom")),
        P(("rep", "dom")),
        P(None, ("rep", "dom")),
        P(),
        P(),
        P(),
        P(),
        P(),
        P(),
        P(),
        P(),
        P(),
    )
    out_specs = P(None, ("rep", "dom"))
    return jax.shard_map(shards, mesh=mesh, in_specs=in_specs, out_specs=out_specs, check_vma=False)
```

profile of v0, /device:TPU:0, one launch (start us, length us, event | category | flops | bytes accessed | tf_op | source)
XLA Modules:
  0.0 50.4 jit_solution(8547945733508768784)
XLA Ops:
  0.7 0.0 copy-start.1
  0.7 0.0 copy-start.2
  0.7 0.0 copy-start.3
  0.7 1.8 %prep.1 = (f32[320,128]{1,0:T(8,128)}, f32[4,128]{1,0:T(4,128)}, f32[4,128]{1,0:T(4,128)}, f32[4,128]{1,0:T(4,128)}, f32[8,128]{1,0:T(8,128)}) custom-call(f32[8]{0:T(128)} %zeta_table.1, f32[8]{0:T(128)} %escale.1, s32[1]{0:T(128)S(6)} %copy.15.live, f32[3,1024]{1,0:T(4,128)} %pos.1, s32[1,1024]{1,0:T(1,128)} %bitcast.11, s32[6,128]{1,0:T(8,128)} %ghost_index.3, ...), custom_call_target="tpu_custom_call" | custom-call | tf_op jit(solution)/shard_map/prep/pallas_call | solution.py:636
  2.5 0.0 copy-start.11
  2.5 0.5 %collective-permute-start = (f32[320,128]{1,0:T(8,128)}, f32[320,128]{1,0:T(8,128)S(1)}, u32[]{:S(2)}, u32[]{:S(2)}) collective-permute-start(f32[320,128]{1,0:T(8,128)} %get-tuple-element.27.pack), channel_id=1, source_target_pairs={{0,1},{1,0},{2,3},{3,2},{4,5},{5,4},{6,7},{7,6},{8,9},{9,8},{10,11... | collective-permute-start | bytes 491528 | tf_op jit(solution)/shard_map/ppermute | solution.py:30
  3.0 0.0 copy-start.10
  3.0 3.7 %collective-permute-start.4 = (f32[8,128]{1,0:T(8,128)}, f32[8,128]{1,0:T(8,128)S(1)}, u32[]{:S(2)}, u32[]{:S(2)}) collective-permute-start(f32[8,128]{1,0:T(8,128)} %get-tuple-element.34), channel_id=1, source_target_pairs={{0,8},{1,9},{2,10},{3,11},{4,12},{5,13},{6,14},{7,15},{8,0},{9,1},... | collective-permute-start | bytes 12296 | tf_op jit(solution)/shard_map/ppermute | solution.py:30
  6.6 0.0 copy-done.11
  6.6 0.0 copy-start.9
  6.7 2.1 %collective-permute-start.1 = (f32[4,128]{1,0:T(4,128)S(1)}, f32[4,128]{1,0:T(4,128)S(1)}, u32[]{:S(2)}, u32[]{:S(2)}) collective-permute-start(f32[4,128]{1,0:T(4,128)S(1)} %copy-done.11), channel_id=1, source_target_pairs={{0,15},{1,2},{2,1},{3,4},{4,3},{5,6},{6,5},{7,8},{8,7},{9,10},{10,... | collective-permute-start | bytes 6152 | tf_op jit(solution)/shard_map/ppermute | solution.py:30
  8.7 0.0 copy-done.10
  8.7 0.0 collective-permute-start.2
  8.7 0.0 copy-start.6
  8.7 0.0 copy-done.9
  8.7 0.0 copy-start.5
  8.7 1.9 %collective-permute-start.3 = (f32[4,128]{1,0:T(4,128)S(1)}, f32[4,128]{1,0:T(4,128)S(1)}, u32[]{:S(2)}, u32[]{:S(2)}) collective-permute-start(f32[4,128]{1,0:T(4,128)S(1)} %copy-done.9), channel_id=1, source_target_pairs={{0,14},{1,15},{2,4},{3,5},{4,2},{5,3},{6,8},{7,9},{8,6},{9,7},{10,... | collective-permute-start | bytes 6152 | tf_op jit(solution)/shard_map/ppermute | solution.py:30
  10.6 0.0 copy-start.7
  10.6 0.0 copy-start.8
  10.6 0.0 copy-done.1
  10.6 0.0 copy-done.2
  10.7 0.0 copy-done.3
  10.7 0.0 copy-done.6
  10.7 0.0 copy-done.5
  10.7 0.6 %copy-done.7 = f32[64]{0:T(128)S(1)} copy-done((f32[64]{0:T(128)S(1)}, f32[64]{0:T(128)}, u32[]{:S(2)}) %copy-start.7) | copy-done | bytes 280
  11.3 0.0 copy-done.8
  11.3 0.0 copy-start
  11.3 0.9 %copy-done = f32[320,128]{1,0:T(8,128)S(1)} copy-done((f32[320,128]{1,0:T(8,128)S(1)}, f32[320,128]{1,0:T(8,128)}, u32[]{:S(2)}) %copy-start) | copy-done | bytes 163864
  12.2 0.4 weights.1
  12.6 0.0 collective-permute-done.1.refs_0_
  12.6 0.0 collective-permute-done.2.refs_1_
  12.6 2.5 %collective-permute-done.3.refs_2_ = f32[4,128]{1,0:T(4,128)S(1)} collective-permute-done((f32[4,128]{1,0:T(4,128)S(1)}, f32[4,128]{1,0:T(4,128)S(1)}, u32[]{:S(2)}, u32[]{:S(2)}) %collective-permute-start.3) | collective-permute-done | bytes 2080 | tf_op jit(solution)/shard_map/ppermute | solution.py:30
  15.1 0.0 collective-permute-done.4.refs_3_
  15.1 0.0 collective-permute-done.mate
  15.1 13.2 %edges.1 = (f32[3,1024]{1,0:T(4,128)S(1)}, f32[32,128]{1,0:T(8,128)S(1)}, f32[4,128]{1,0:T(4,128)S(1)}, f32[4,128]{1,0:T(4,128)S(1)}, f32[4,128]{1,0:T(4,128)S(1)}, /*index=5*/f32[8,128]{1,0:T(8,128)S(1)}) custom-call(s32[1]{0:T(128)S(6)} %copy.15.live, f32[320,128]{1,0:T(8,128)S(1)} %get-tuple-element.28.pack, f32[320,128]{1,0:T(8,128)S(1)} %collective-permute-done.mate, ...), custom_call_target="tpu_custom_call" | custom-call | tf_op jit(solution)/shard_map/edges/pallas_call | solution.py:668
  28.3 0.1 collective-permute-start.5
  28.4 0.0 copy-start.4
  28.4 4.3 %collective-permute-start.9 = (f32[8,128]{1,0:T(8,128)S(1)}, f32[8,128]{1,0:T(8,128)S(1)}, u32[]{:S(2)}, u32[]{:S(2)}) collective-permute-start(f32[8,128]{1,0:T(8,128)S(1)} %get-tuple-element.48), channel_id=1, source_target_pairs={{0,8},{1,9},{2,10},{3,11},{4,12},{5,13},{6,14},{7,15},{8,0},{9,1},... | collective-permute-start | bytes 12296 | tf_op jit(solution)/shard_map/ppermute | solution.py:30
  32.6 10.6 %collective-permute-start.6 = (f32[4,128]{1,0:T(4,128)S(1)}, f32[4,128]{1,0:T(4,128)S(1)}, u32[]{:S(2)}, u32[]{:S(2)}) collective-permute-start(f32[4,128]{1,0:T(4,128)S(1)} %get-tuple-element.45), channel_id=1, source_target_pairs={{0,15},{1,2},{2,1},{3,4},{4,3},{5,6},{6,5},{7,8},{8,7},{9,10},{10,... | collective-permute-start | bytes 6152 | tf_op jit(solution)/shard_map/ppermute | solution.py:30
  43.3 0.0 collective-permute-start.7
  43.3 0.2 collective-permute-start.8
  43.5 1.1 %collective-permute-done.6.refs_0_ = f32[4,128]{1,0:T(4,128)S(1)} collective-permute-done((f32[4,128]{1,0:T(4,128)S(1)}, f32[4,128]{1,0:T(4,128)S(1)}, u32[]{:S(2)}, u32[]{:S(2)}) %collective-permute-start.6) | collective-permute-done | bytes 2080 | tf_op jit(solution)/shard_map/ppermute | solution.py:30
  44.6 2.3 %collective-permute-done.7.refs_1_ = f32[4,128]{1,0:T(4,128)S(1)} collective-permute-done((f32[4,128]{1,0:T(4,128)S(1)}, f32[4,128]{1,0:T(4,128)S(1)}, u32[]{:S(2)}, u32[]{:S(2)}) %collective-permute-start.7) | collective-permute-done | bytes 2080 | tf_op jit(solution)/shard_map/ppermute | solution.py:30
  46.8 2.7 %collective-permute-done.8.refs_2_ = f32[4,128]{1,0:T(4,128)S(1)} collective-permute-done((f32[4,128]{1,0:T(4,128)S(1)}, f32[4,128]{1,0:T(4,128)S(1)}, u32[]{:S(2)}, u32[]{:S(2)}) %collective-permute-start.8) | collective-permute-done | bytes 2080 | tf_op jit(solution)/shard_map/ppermute | solution.py:30
  49.5 0.0 collective-permute-done.9.refs_3_
  49.5 0.0 collective-permute-done.5.back
  49.5 0.0 copy-done.4
  49.6 0.8 %fold.1 = f32[3,1024]{1,0:T(4,128)} custom-call(f32[3,1024]{1,0:T(4,128)S(1)} %get-tuple-element.43.own, f32[32,128]{1,0:T(8,128)S(1)} %collective-permute-done.5.back, s32[6,128]{1,0:T(8,128)S(1)} %copy-done.4, f32[4,128]{1,0:T(4,128)S(1)} %collective-permute-done.6.refs_0_, f32[4,128]{1,0:T(4,128)S(1)} %collective-permute-done.7.refs_1_, ...), custom_call_target="tpu_custom_call" | custom-call | tf_op jit(solution)/shard_map/fold/pallas_call | solution.py:695
Async XLA Ops:
  0.7 10.0 %copy-start.1 = (f32[64,64]{1,0:T(8,128)S(1)}, f32[64,64]{1,0:T(8,128)}, u32[]{:S(2)}) copy-start(f32[64,64]{1,0:T(8,128)} %latent.1) | copy-start | bytes 49156
  0.7 10.0 %copy-start.2 = (f32[64,64]{1,0:T(8,128)S(1)}, f32[64,64]{1,0:T(8,128)}, u32[]{:S(2)}) copy-start(f32[64,64]{1,0:T(8,128)} %env.1) | copy-start | bytes 49156
  0.7 10.0 %copy-start.3 = (f32[64,128]{1,0:T(8,128)S(1)}, f32[64,128]{1,0:T(8,128)}, u32[]{:S(2)}) copy-start(f32[64,128]{1,0:T(8,128)} %mix.1) | copy-start | bytes 98308
  2.5 4.2 %copy-start.11 = (f32[4,128]{1,0:T(4,128)S(1)}, f32[4,128]{1,0:T(4,128)}, u32[]{:S(2)}) copy-start(f32[4,128]{1,0:T(4,128)} %get-tuple-element.31) | copy-start | bytes 6148
  2.5 12.6 %collective-permute-start = (f32[320,128]{1,0:T(8,128)}, f32[320,128]{1,0:T(8,128)S(1)}, u32[]{:S(2)}, u32[]{:S(2)}) collective-permute-start(f32[320,128]{1,0:T(8,128)} %get-tuple-element.27.pack), channel_id=1, source_target_pairs={{0,1},{1,0},{2,3},{3,2},{4,5},{5,4},{6,7},{7,6},{8,9},{9,8},{10,11... | collective-permute-start | bytes 491528 | tf_op jit(solution)/shard_map/ppermute | solution.py:30
  3.0 5.7 %copy-start.10 = (f32[4,128]{1,0:T(4,128)S(1)}, f32[4,128]{1,0:T(4,128)}, u32[]{:S(2)}) copy-start(f32[4,128]{1,0:T(4,128)} %get-tuple-element.32) | copy-start | bytes 6148
  3.0 12.1 %collective-permute-start.4 = (f32[8,128]{1,0:T(8,128)}, f32[8,128]{1,0:T(8,128)S(1)}, u32[]{:S(2)}, u32[]{:S(2)}) collective-permute-start(f32[8,128]{1,0:T(8,128)} %get-tuple-element.34), channel_id=1, source_target_pairs={{0,8},{1,9},{2,10},{3,11},{4,12},{5,13},{6,14},{7,15},{8,0},{9,1},... | collective-permute-start | bytes 12296 | tf_op jit(solution)/shard_map/ppermute | solution.py:30
  6.6 2.1 %copy-start.9 = (f32[4,128]{1,0:T(4,128)S(1)}, f32[4,128]{1,0:T(4,128)}, u32[]{:S(2)}) copy-start(f32[4,128]{1,0:T(4,128)} %get-tuple-element.33) | copy-start | bytes 6148
  6.7 6.0 %collective-permute-start.1 = (f32[4,128]{1,0:T(4,128)S(1)}, f32[4,128]{1,0:T(4,128)S(1)}, u32[]{:S(2)}, u32[]{:S(2)}) collective-permute-start(f32[4,128]{1,0:T(4,128)S(1)} %copy-done.11), channel_id=1, source_target_pairs={{0,15},{1,2},{2,1},{3,4},{4,3},{5,6},{6,5},{7,8},{8,7},{9,10},{10,... | collective-permute-start | bytes 6152 | tf_op jit(solution)/shard_map/ppermute | solution.py:30
  8.7 3.9 %collective-permute-start.2 = (f32[4,128]{1,0:T(4,128)S(1)}, f32[4,128]{1,0:T(4,128)S(1)}, u32[]{:S(2)}, u32[]{:S(2)}) collective-permute-start(f32[4,128]{1,0:T(4,128)S(1)} %copy-done.10), channel_id=1, source_target_pairs={{0,2},{1,3},{2,0},{3,1},{4,6},{5,7},{6,4},{7,5},{8,10},{9,11},{10,... | collective-permute-start | bytes 6152 | tf_op jit(solution)/shard_map/ppermute | solution.py:30
  8.7 1.9 %copy-start.6 = (f32[64,8]{0,1:T(8,128)S(1)}, f32[64,8]{0,1:T(8,128)}, u32[]{:S(2)}) copy-start(f32[64,8]{0,1:T(8,128)} %param.23) | copy-start | bytes 6148
  8.7 1.9 %copy-start.5 = (f32[64,8]{0,1:T(8,128)S(1)}, f32[64,8]{0,1:T(8,128)}, u32[]{:S(2)}) copy-start(f32[64,8]{0,1:T(8,128)} %param.21) | copy-start | bytes 6148
  8.7 6.3 %collective-permute-start.3 = (f32[4,128]{1,0:T(4,128)S(1)}, f32[4,128]{1,0:T(4,128)S(1)}, u32[]{:S(2)}, u32[]{:S(2)}) collective-permute-start(f32[4,128]{1,0:T(4,128)S(1)} %copy-done.9), channel_id=1, source_target_pairs={{0,14},{1,15},{2,4},{3,5},{4,2},{5,3},{6,8},{7,9},{8,6},{9,7},{10,... | collective-permute-start | bytes 6152 | tf_op jit(solution)/shard_map/ppermute | solution.py:30
  10.6 0.7 %copy-start.7 = (f32[64]{0:T(128)S(1)}, f32[64]{0:T(128)}, u32[]{:S(2)}) copy-start(f32[64]{0:T(128)} %param.22) | copy-start | bytes 772
  10.6 0.7 %copy-start.8 = (f32[64]{0:T(128)S(1)}, f32[64]{0:T(128)}, u32[]{:S(2)}) copy-start(f32[64]{0:T(128)} %param.27) | copy-start | bytes 772
  11.3 0.9 %copy-start = (f32[320,128]{1,0:T(8,128)S(1)}, f32[320,128]{1,0:T(8,128)}, u32[]{:S(2)}) copy-start(f32[320,128]{1,0:T(8,128)} %get-tuple-element.27.pack) | copy-start | bytes 491524
  28.3 21.2 %collective-permute-start.5 = (f32[32,128]{1,0:T(8,128)S(1)}, f32[32,128]{1,0:T(8,128)S(1)}, u32[]{:S(2)}, u32[]{:S(2)}) collective-permute-start(f32[32,128]{1,0:T(8,128)S(1)} %get-tuple-element.44), channel_id=1, source_target_pairs={{0,1},{1,0},{2,3},{3,2},{4,5},{5,4},{6,7},{7,6},{8,9},{9,8},{10,11... | collective-permute-start | bytes 49160 | tf_op jit(solution)/shard_map/ppermute | solution.py:30
  28.4 21.2 %copy-start.4 = (s32[6,128]{1,0:T(8,128)S(1)}, s32[6,128]{1,0:T(8,128)}, u32[]{:S(2)}) copy-start(s32[6,128]{1,0:T(8,128)} %ghost_index.3) | copy-start | bytes 9220
  28.4 21.2 %collective-permute-start.9 = (f32[8,128]{1,0:T(8,128)S(1)}, f32[8,128]{1,0:T(8,128)S(1)}, u32[]{:S(2)}, u32[]{:S(2)}) collective-permute-start(f32[8,128]{1,0:T(8,128)S(1)} %get-tuple-element.48), channel_id=1, source_target_pairs={{0,8},{1,9},{2,10},{3,11},{4,12},{5,13},{6,14},{7,15},{8,0},{9,1},... | collective-permute-start | bytes 12296 | tf_op jit(solution)/shard_map/ppermute | solution.py:30
  32.6 11.9 %collective-permute-start.6 = (f32[4,128]{1,0:T(4,128)S(1)}, f32[4,128]{1,0:T(4,128)S(1)}, u32[]{:S(2)}, u32[]{:S(2)}) collective-permute-start(f32[4,128]{1,0:T(4,128)S(1)} %get-tuple-element.45), channel_id=1, source_target_pairs={{0,15},{1,2},{2,1},{3,4},{4,3},{5,6},{6,5},{7,8},{8,7},{9,10},{10,... | collective-permute-start | bytes 6152 | tf_op jit(solution)/shard_map/ppermute | solution.py:30
  43.3 3.6 %collective-permute-start.7 = (f32[4,128]{1,0:T(4,128)S(1)}, f32[4,128]{1,0:T(4,128)S(1)}, u32[]{:S(2)}, u32[]{:S(2)}) collective-permute-start(f32[4,128]{1,0:T(4,128)S(1)} %get-tuple-element.46), channel_id=1, source_target_pairs={{0,2},{1,3},{2,0},{3,1},{4,6},{5,7},{6,4},{7,5},{8,10},{9,11},{10,... | collective-permute-start | bytes 6152 | tf_op jit(solution)/shard_map/ppermute | solution.py:30
  43.3 6.3 %collective-permute-start.8 = (f32[4,128]{1,0:T(4,128)S(1)}, f32[4,128]{1,0:T(4,128)S(1)}, u32[]{:S(2)}, u32[]{:S(2)}) collective-permute-start(f32[4,128]{1,0:T(4,128)S(1)} %get-tuple-element.47), channel_id=1, source_target_pairs={{0,14},{1,15},{2,4},{3,5},{4,2},{5,3},{6,8},{7,9},{8,6},{9,7},{10,... | collective-permute-start | bytes 6152 | tf_op jit(solution)/shard_map/ppermute | solution.py:30
where the time goes:
time: 50.6 us; the launch traced here: 50.4 us
  starting transfers between devices  23.3 us (46%)
  Pallas kernels  16.2 us (32%)
  waiting for transfers between devices  8.55 us (17%)
  local copies, waits for them, and re-layouts  1.59 us (3%)
  between operations  0.77 us (2%)
    ppermute x10, starting transfers between devices, swap(): return lax.ppermute(block, 'dom', [(i, partner(i)) for i in range(size)])  23.3 us
    pallas_call x1, Pallas kernels, shards(): pl.pallas_call(functools.partial(edge_kernel, steps=steps, batch=8, lag=1...  13.2 us
    ppermute x10, waiting for transfers between devices, swap(): return lax.ppermute(block, 'dom', [(i, partner(i)) for i in range(size)])  8.55 us
    pallas_call x1, Pallas kernels, shards(): pl.pallas_call(functools.partial(prep_kernel, steps=steps), out_shape=[sh...  1.78 us
    unnamed x24, local copies, waits for them, and re-layouts  1.59 us
  transfers between devices with their start and end apart: 10, of which 4 were waited for; matrix products, arithmetic and copies ran while one was open for 0% of the time, Pallas kernels for 1%

commit v1 on v0

--- a/solution.py
+++ b/solution.py
@@ -188,10 +188,13 @@
     ghost_out = refs[nsends + 10 : 2 * nsends + 10]
     (
         table,
+        lists,
         index_s,
+        keep_s,
         basis_s,
         kinds_s,
         geo_s,
+        force_s,
         red_s,
         outf_s,
         db_s,
@@ -214,6 +217,9 @@
     for t in range(own_tiles):
         table[0, t] = pack[8 * t : 8 * t + 8, :]
         table[1, t] = mate[8 * t : 8 * t + 8, :]
+    edge_rows = pack.shape[0] - 8 * own_tiles
+    lists[:edge_rows, :] = pack[8 * own_tiles :, :]
+    lists[edge_rows:, :] = mate[8 * own_tiles :, :]
     for a, step in enumerate(steps):
         par = parity(step)
         for flip in range(2):
@@ -227,6 +233,8 @@
                 table[0, tile, d : d + 1, :] = row
     acc_s[...] = jnp.zeros(acc_s.shape, F32)
     own_s[...] = jnp.zeros(own_s.shape, F32)
+    for ref in (keep_s, index_s, red_s, outf_s, db_s):
+        ref[...] = jnp.zeros(ref.shape, F32)
 
     w1, w2, w3, w4, w5, w6, w7, w8 = [ref[...] for ref in weights]
     out_row2 = row2[...]
@@ -236,6 +244,8 @@
     from_lane = lax.broadcasted_iota(jnp.int32, (LANES, LANES), 0)
     to_lane = lax.broadcasted_iota(jnp.int32, (LANES, LANES), 1)
     per_row = LANES // NBR
+    lane_bf = from_lane.astype(F32).astype(BF16)
+    one_bf, zero_bf = jnp.ones((), BF16), jnp.zeros((), BF16)
     sel_s[...] = jnp.where(from_lane // NBR == to_lane % per_row, 1.0, 0.0).astype(BF16)
     sub8 = lax.broadcasted_iota(jnp.int32, (8, LANES), 0)
     lane8 = lax.broadcasted_iota(jnp.int32, (8, LANES), 1)
@@ -261,7 +271,74 @@
     def slope2(u, f):
         return u + f * (2.0 - u)
 
+    def finish(which, kb, odd):
+        index = index_s[...].astype(jnp.int32)
+        low, high = index & (LANES - 1), index >> 7
+        local = 2 * sub8 + odd
+        upper = sub8 < 4
+        kept = [keep_s[q] for q in range(keep_s.shape[0])]
+        sins, coss, unit = kept[:nb], kept[nb : 2 * nb], kept[2 * nb : 2 * nb + 3]
+        envelope, x, inv_x, gap, inv_dist, scale_of, occupied = kept[2 * nb + 3 :]
+
+        def collect(ref, q):
+            total = ref[q, pl.ds(0, NBR, stride=8), :]
+            for k in range(1, 8):
+                total = total + ref[q, pl.ds(k, NBR, stride=8), :]
+            return total
+
+        pulls = [collect(red_s, 3 + d) for d in range(3)]
+        d_unit = [envelope * (collect(red_s, d) + pulls[d]) for d in range(3)]
+        d_env = collect(red_s, 6) + outf_s[...]
+        for d in range(3):
+            d_env = d_env + unit[d] * pulls[d]
+        along = jnp.zeros((NBR, LANES), F32)
+        level = jnp.zeros((NBR, LANES), F32)
+        for k in range(nb):
+            g = db_s[pl.ds(k, NBR, stride=8), :]
+            ratio = sins[k] * inv_x
+            level = level + g * ratio
+            along = along + g * ((k + 1) * math.pi * coss[k] - ratio)
+        d_env = d_env + envelope * level
+        d_x = envelope * envelope * inv_x * along - 4.0 * x * gap * d_env
+        radial = d_x * (1.0 / CUTOFF)
+        for d in range(3):
+            radial = radial - d_unit[d] * unit[d] * inv_dist
+        lefts = []
+        for d in range(3):
+            g = jnp.where(occupied > 0.0, (d_unit[d] * inv_dist + radial * unit[d]) * scale_of, 0.0)
+            top = g.astype(BF16).astype(F32)
+            force_s[2 * d] = top
+            force_s[2 * d + 1] = g - top
+            lefts += [top, g - top]
+        sums = mm(jnp.concatenate(lefts, axis=0).astype(BF16), sel_s[...])
+        own_rows = []
+        for d in range(3):
+            total = jnp.zeros((8, LANES), F32)
+            for part in range(4):
+                row = 64 * d + 8 * part
+                value = sums[row : row + 8] + sums[row + NBR : row + NBR + 8]
+                total = total + jnp.where((lane8 % BIN_ATOMS) // per_row == part, value, 0.0)
+            total = jnp.where(lane8 // BIN_ATOMS == local % group, total, 0.0)
+            for h in range(2):
+                own_rows.append(jnp.sum(jnp.where(upper == (h == 0), total, 0.0), axis=0, keepdims=True))
+        for d in range(3):
+            for h in range(2):
+                own_s[which, d, pl.ds(2 * kb + h, 1), :] += own_rows[2 * d + h]
+
+        lefts, rights = [], []
+        index_s[...] = low.astype(F32)
+        for n in range(NBR):
+            highs = high[n : n + 1]
+            lows = jnp.broadcast_to(index_s[n : n + 1, :], (16, LANES)).astype(BF16)
+            lows = jnp.concatenate([lows] * (LANES // 16), axis=0)
+            rights.append(jnp.where(lane_bf == lows, one_bf, zero_bf))
+            hit = sub16 == highs
+            rows = [jnp.where(hit, force_s[q, n : n + 1, :], 0.0) for q in range(6)]
+            lefts.append(jnp.concatenate(rows, axis=0).astype(BF16))
+        acc_s[which] += mm_nt(jnp.concatenate(lefts, axis=1), jnp.concatenate(rights, axis=1))
+
     def block(i, carry):
+        finish(*carry)
         is_mate = i >= keep_even + my_odd
         is_odd = jnp.logical_and(i >= keep_even, jnp.logical_not(is_mate))
         which = jnp.where(is_mate, 1, 0)
@@ -270,21 +347,11 @@
             is_mate, their_even - take + i - keep_even - my_odd, jnp.where(is_odd, i - keep_even, i)
         )
         bins = jnp.where(is_mate, theirs, mine)
-        row0 = pl.multiple_of(64 * kb, 64)
-
-        @pl.when(is_mate)
-        def _():
-            for part in range(4):
-                got = mate[pl.ds(8 * own_tiles + row0 + part, 8, stride=8), :]
-                index_s[8 * part : 8 * part + 8, :] = got
-
-        @pl.when(jnp.logical_not(is_mate))
-        def _():
-            for part in range(4):
-                start = 8 * own_tiles + row0 + 4 * odd + part
-                index_s[8 * part : 8 * part + 8, :] = pack[pl.ds(start, 8, stride=8), :]
-
-        index = index_s[...].astype(jnp.int32)
+        start = edge_rows * which + 64 * kb + 4 * odd
+        rows = [lists[pl.ds(start + part, 8, stride=8), :] for part in range(4)]
+        index = jnp.concatenate(rows, axis=0)
+        index_s[...] = index
+        index = index.astype(jnp.int32)
         low, high = index & (LANES - 1), index >> 7
 
         local = 2 * sub8 + odd
@@ -478,9 +545,9 @@
             stage_mix,
             stage_third,
             stage_denv,
+            stage_pull,
             stage_back,
             stage_slope2,
-            stage_pull,
             stage_slope1,
         ]
         groups = [range(t0, t0 + batch) for t0 in range(0, NBR // 2, batch)]
@@ -489,62 +556,13 @@
                 if 0 <= turn - i * lag < len(stages):
                     stages[turn - i * lag](ts)
 
-        def collect(ref, q):
-            total = ref[q, pl.ds(0, NBR, stride=8), :]
-            for k in range(1, 8):
-                total = total + ref[q, pl.ds(k, NBR, stride=8), :]
-            return total
-
-        pulls = [collect(red_s, 3 + d) for d in range(3)]
-        d_unit = [envelope * (collect(red_s, d) + pulls[d]) for d in range(3)]
-        d_env = collect(red_s, 6) + outf_s[...]
-        for d in range(3):
-            d_env = d_env + unit[d] * pulls[d]
-        along = jnp.zeros((NBR, LANES), F32)
-        level = jnp.zeros((NBR, LANES), F32)
-        for k in range(nb):
-            g = db_s[pl.ds(k, NBR, stride=8), :]
-            ratio = sins[k] * inv_x
-            level = level + g * ratio
-            along = along + g * ((k + 1) * math.pi * coss[k] - ratio)
-        d_env = d_env + envelope * level
-        d_x = envelope * envelope * inv_x * along - 4.0 * x * gap * d_env
-        radial = d_x * (1.0 / CUTOFF)
-        for d in range(3):
-            radial = radial - d_unit[d] * unit[d] * inv_dist
-        lefts = []
-        for d in range(3):
-            g = jnp.where(occupied > 0.0, (d_unit[d] * inv_dist + radial * unit[d]) * here[4], 0.0)
-            top = g.astype(BF16).astype(F32)
-            geo_s[2 * d] = top
-            geo_s[2 * d + 1] = g - top
-            lefts += [top, g - top]
-        sums = mm(jnp.concatenate(lefts, axis=0).astype(BF16), sel_s[...])
-        own_rows = []
-        for d in range(3):
-            total = jnp.zeros((8, LANES), F32)
-            for part in range(4):
-                row = 64 * d + 8 * part
-                value = sums[row : row + 8] + sums[row + NBR : row + NBR + 8]
-                total = total + jnp.where((lane8 % BIN_ATOMS) // per_row == part, value, 0.0)
-            total = jnp.where(lane8 // BIN_ATOMS == local % group, total, 0.0)
-            for h in range(2):
-                own_rows.append(jnp.sum(jnp.where(upper == (h == 0), total, 0.0), axis=0, keepdims=True))
-        for d in range(3):
-            for h in range(2):
-                own_s[which, d, pl.ds(2 * kb + h, 1), :] += own_rows[2 * d + h]
-
-        lefts, rights = [], []
-        for n in range(NBR):
-            lows, highs = low[n : n + 1], high[n : n + 1]
-            rights.append(jnp.where(from_lane == lows, 1.0, 0.0).astype(BF16))
-            hit = sub16 == highs
-            rows = [jnp.where(hit, geo_s[q, n : n + 1, :], 0.0) for q in range(6)]
-            lefts.append(jnp.concatenate(rows, axis=0).astype(BF16))
-        acc_s[which] += mm_nt(jnp.concatenate(lefts, axis=1), jnp.concatenate(rights, axis=1))
-        return carry
-
-    lax.fori_loop(0, keep_even + my_odd + take, block, 0)
+        for q, value in enumerate([*sins, *coss, *unit, envelope, x, inv_x, gap, inv_dist, here[4], occupied]):
+            keep_s[q] = value
+        return which, kb, odd
+
+    zero = jnp.int32(0)
+    last = lax.fori_loop(0, keep_even + my_odd + take, block, (zero, zero, zero))
+    finish(*last)
 
     for d in range(3):
         for which in range(2):
@@ -672,10 +690,13 @@
         out_specs=[VM()] * (2 + len(buffers)),
         scratch_shapes=[
             pltpu.VMEM((2, 16, 8, LANES), F32),
+            pltpu.VMEM((2 * nbr.shape[0], LANES), F32),
             pltpu.VMEM((NBR, LANES), F32),
+            pltpu.VMEM((2 * radial_weight.shape[1] + 10, NBR, LANES), F32),
             pltpu.VMEM((NBR * 16, LANES), F32),
             pltpu.VMEM((NBR, LANES), F32),
             pltpu.VMEM((12, NBR, LANES), F32),
+            pltpu.VMEM((6, NBR, LANES), F32),
             pltpu.VMEM((7, NBR * 8, LANES), F32),
             pltpu.VMEM((NBR, LANES), F32),
             pltpu.VMEM((NBR * 8, LANES), F32),

time: 50.6 us -> 49 us (0.968)
  Pallas kernels: 16.2 us -> 27.5 us
  starting transfers between devices: 23.3 us -> 13.5 us
  waiting for transfers between devices: 8.55 us -> 5.62 us
    pallas_call x1, Pallas kernels: 13.2 us -> 24.5 us  [shards(): pl.pallas_call(functools.partial(edge_kernel, steps=steps, batch=8, lag=1...]
    ppermute x10, starting transfers between devices: 23.3 us -> 13.5 us  [swap(): return lax.ppermute(block, 'dom', [(i, partner(i)) for i in range(size)])]
    ppermute x10, waiting for transfers between devices: 8.55 us -> 5.62 us  [swap(): return lax.ppermute(block, 'dom', [(i, partner(i)) for i in range(size)])]
  transfers between devices with their start and end apart: 10 -> 10, of which waited for: 4 -> 3; matrix products, arithmetic and copies ran while one was open for 0% -> 0% of each run, Pallas kernels for 1% -> 1%
where the time goes in v1:
time: 49 us; the launch traced here: 48.9 us
  Pallas kernels  27.5 us (56%)
  starting transfers between devices  13.5 us (28%)
  waiting for transfers between devices  5.62 us (11%)
  local copies, waits for them, and re-layouts  1.59 us (3%)
  between operations  0.79 us (2%)
    pallas_call x1, Pallas kernels, shards(): pl.pallas_call(functools.partial(edge_kernel, steps=steps, batch=8, lag=1...  24.5 us
    ppermute x10, starting transfers between devices, swap(): return lax.ppermute(block, 'dom', [(i, partner(i)) for i in range(size)])  13.5 us
    ppermute x10, waiting for transfers between devices, swap(): return lax.ppermute(block, 'dom', [(i, partner(i)) for i in range(size)])  5.62 us
    pallas_call x1, Pallas kernels, shards(): pl.pallas_call(functools.partial(prep_kernel, steps=steps), out_shape=[sh...  1.78 us
    unnamed x24, local copies, waits for them, and re-layouts  1.59 us
  transfers between devices with their start and end apart: 10, of which 3 were waited for; matrix products, arithmetic and copies ran while one was open for 0% of the time, Pallas kernels for 1%

profile of v1, /device:TPU:0, one launch (start us, length us, event | category | flops | bytes accessed | tf_op | source)
XLA Modules:
  0.0 48.9 jit_solution(16120112012162025841)
XLA Ops:
  0.7 0.0 copy-start.1
  0.7 0.0 copy-start.2
  0.7 0.0 copy-start.3
  0.7 1.8 %prep.1 = (f32[320,128]{1,0:T(8,128)}, f32[4,128]{1,0:T(4,128)}, f32[4,128]{1,0:T(4,128)}, f32[4,128]{1,0:T(4,128)}, f32[8,128]{1,0:T(8,128)}) custom-call(f32[8]{0:T(128)} %zeta_table.1, f32[8]{0:T(128)} %escale.1, s32[1]{0:T(128)S(6)} %copy.15.live, f32[3,1024]{1,0:T(4,128)} %pos.1, s32[1,1024]{1,0:T(1,128)} %bitcast.11, s32[6,128]{1,0:T(8,128)} %ghost_index.3, ...), custom_call_target="tpu_custom_call" | custom-call | tf_op jit(solution)/shard_map/prep/pallas_call | solution.py:654
  2.5 0.0 copy-start.11
  2.5 0.5 %collective-permute-start = (f32[320,128]{1,0:T(8,128)}, f32[320,128]{1,0:T(8,128)S(1)}, u32[]{:S(2)}, u32[]{:S(2)}) collective-permute-start(f32[320,128]{1,0:T(8,128)} %get-tuple-element.27.pack), channel_id=1, source_target_pairs={{0,1},{1,0},{2,3},{3,2},{4,5},{5,4},{6,7},{7,6},{8,9},{9,8},{10,11... | collective-permute-start | bytes 491528 | tf_op jit(solution)/shard_map/ppermute | solution.py:30
  3.0 0.0 copy-start.10
  3.0 3.7 %collective-permute-start.4 = (f32[8,128]{1,0:T(8,128)}, f32[8,128]{1,0:T(8,128)S(1)}, u32[]{:S(2)}, u32[]{:S(2)}) collective-permute-start(f32[8,128]{1,0:T(8,128)} %get-tuple-element.34), channel_id=1, source_target_pairs={{0,8},{1,9},{2,10},{3,11},{4,12},{5,13},{6,14},{7,15},{8,0},{9,1},... | collective-permute-start | bytes 12296 | tf_op jit(solution)/shard_map/ppermute | solution.py:30
  6.6 0.0 copy-done.11
  6.6 0.0 copy-start.9
  6.7 2.1 %collective-permute-start.1 = (f32[4,128]{1,0:T(4,128)S(1)}, f32[4,128]{1,0:T(4,128)S(1)}, u32[]{:S(2)}, u32[]{:S(2)}) collective-permute-start(f32[4,128]{1,0:T(4,128)S(1)} %copy-done.11), channel_id=1, source_target_pairs={{0,15},{1,2},{2,1},{3,4},{4,3},{5,6},{6,5},{7,8},{8,7},{9,10},{10,... | collective-permute-start | bytes 6152 | tf_op jit(solution)/shard_map/ppermute | solution.py:30
  8.7 0.0 copy-done.10
  8.7 0.0 collective-permute-start.2
  8.7 0.0 copy-start.6
  8.7 0.0 copy-done.9
  8.7 0.0 copy-start.5
  8.7 1.9 %collective-permute-start.3 = (f32[4,128]{1,0:T(4,128)S(1)}, f32[4,128]{1,0:T(4,128)S(1)}, u32[]{:S(2)}, u32[]{:S(2)}) collective-permute-start(f32[4,128]{1,0:T(4,128)S(1)} %copy-done.9), channel_id=1, source_target_pairs={{0,14},{1,15},{2,4},{3,5},{4,2},{5,3},{6,8},{7,9},{8,6},{9,7},{10,... | collective-permute-start | bytes 6152 | tf_op jit(solution)/shard_map/ppermute | solution.py:30
  10.6 0.0 copy-start.7
  10.6 0.0 copy-start.8
  10.6 0.0 copy-done.1
  10.6 0.0 copy-done.2
  10.7 0.0 copy-done.3
  10.7 0.0 copy-done.6
  10.7 0.0 copy-done.5
  10.7 0.6 %copy-done.7 = f32[64]{0:T(128)S(1)} copy-done((f32[64]{0:T(128)S(1)}, f32[64]{0:T(128)}, u32[]{:S(2)}) %copy-start.7) | copy-done | bytes 280
  11.3 0.0 copy-done.8
  11.3 0.0 copy-start
  11.3 0.9 %copy-done = f32[320,128]{1,0:T(8,128)S(1)} copy-done((f32[320,128]{1,0:T(8,128)S(1)}, f32[320,128]{1,0:T(8,128)}, u32[]{:S(2)}) %copy-start) | copy-done | bytes 163864
  12.2 0.4 weights.1
  12.6 0.0 collective-permute-done.1.refs_0_
  12.6 0.0 collective-permute-done.2.refs_1_
  12.6 2.5 %collective-permute-done.3.refs_2_ = f32[4,128]{1,0:T(4,128)S(1)} collective-permute-done((f32[4,128]{1,0:T(4,128)S(1)}, f32[4,128]{1,0:T(4,128)S(1)}, u32[]{:S(2)}, u32[]{:S(2)}) %collective-permute-start.3) | collective-permute-done | bytes 2080 | tf_op jit(solution)/shard_map/ppermute | solution.py:30
  15.1 0.0 collective-permute-done.4.refs_3_
  15.1 0.0 collective-permute-done.mate
  15.1 24.5 %edges.1 = (f32[3,1024]{1,0:T(4,128)S(1)}, f32[32,128]{1,0:T(8,128)S(1)}, f32[4,128]{1,0:T(4,128)S(1)}, f32[4,128]{1,0:T(4,128)S(1)}, f32[4,128]{1,0:T(4,128)S(1)}, /*index=5*/f32[8,128]{1,0:T(8,128)S(1)}) custom-call(s32[1]{0:T(128)S(6)} %copy.15.live, f32[320,128]{1,0:T(8,128)S(1)} %get-tuple-element.28.pack, f32[320,128]{1,0:T(8,128)S(1)} %collective-permute-done.mate, ...), custom_call_target="tpu_custom_call" | custom-call | tf_op jit(solution)/shard_map/edges/pallas_call | solution.py:686
  39.6 0.1 collective-permute-start.5
  39.7 0.0 copy-start.4
  39.7 0.1 collective-permute-start.9
  39.8 0.1 collective-permute-start.6
  39.8 2.0 %collective-permute-start.7 = (f32[4,128]{1,0:T(4,128)S(1)}, f32[4,128]{1,0:T(4,128)S(1)}, u32[]{:S(2)}, u32[]{:S(2)}) collective-permute-start(f32[4,128]{1,0:T(4,128)S(1)} %get-tuple-element.46), channel_id=1, source_target_pairs={{0,2},{1,3},{2,0},{3,1},{4,6},{5,7},{6,4},{7,5},{8,10},{9,11},{10,... | collective-permute-start | bytes 6152 | tf_op jit(solution)/shard_map/ppermute | solution.py:30
  41.8 3.1 %collective-permute-start.8 = (f32[4,128]{1,0:T(4,128)S(1)}, f32[4,128]{1,0:T(4,128)S(1)}, u32[]{:S(2)}, u32[]{:S(2)}) collective-permute-start(f32[4,128]{1,0:T(4,128)S(1)} %get-tuple-element.47), channel_id=1, source_target_pairs={{0,14},{1,15},{2,4},{3,5},{4,2},{5,3},{6,8},{7,9},{8,6},{9,7},{10,... | collective-permute-start | bytes 6152 | tf_op jit(solution)/shard_map/ppermute | solution.py:30
  44.9 0.6 %collective-permute-done.6.refs_0_ = f32[4,128]{1,0:T(4,128)S(1)} collective-permute-done((f32[4,128]{1,0:T(4,128)S(1)}, f32[4,128]{1,0:T(4,128)S(1)}, u32[]{:S(2)}, u32[]{:S(2)}) %collective-permute-start.6) | collective-permute-done | bytes 2080 | tf_op jit(solution)/shard_map/ppermute | solution.py:30
  45.5 0.0 collective-permute-done.7.refs_1_
  45.5 2.5 %collective-permute-done.8.refs_2_ = f32[4,128]{1,0:T(4,128)S(1)} collective-permute-done((f32[4,128]{1,0:T(4,128)S(1)}, f32[4,128]{1,0:T(4,128)S(1)}, u32[]{:S(2)}, u32[]{:S(2)}) %collective-permute-start.8) | collective-permute-done | bytes 2080 | tf_op jit(solution)/shard_map/ppermute | solution.py:30
  48.1 0.0 collective-permute-done.9.refs_3_
  48.1 0.0 collective-permute-done.5.back
  48.1 0.0 copy-done.4
  48.1 0.8 %fold.1 = f32[3,1024]{1,0:T(4,128)} custom-call(f32[3,1024]{1,0:T(4,128)S(1)} %get-tuple-element.43.own, f32[32,128]{1,0:T(8,128)S(1)} %collective-permute-done.5.back, s32[6,128]{1,0:T(8,128)S(1)} %copy-done.4, f32[4,128]{1,0:T(4,128)S(1)} %collective-permute-done.6.refs_0_, f32[4,128]{1,0:T(4,128)S(1)} %collective-permute-done.7.refs_1_, ...), custom_call_target="tpu_custom_call" | custom-call | tf_op jit(solution)/shard_map/fold/pallas_call | solution.py:716
Async XLA Ops:
  0.7 10.0 %copy-start.1 = (f32[64,64]{1,0:T(8,128)S(1)}, f32[64,64]{1,0:T(8,128)}, u32[]{:S(2)}) copy-start(f32[64,64]{1,0:T(8,128)} %latent.1) | copy-start | bytes 49156
  0.7 10.0 %copy-start.2 = (f32[64,64]{1,0:T(8,128)S(1)}, f32[64,64]{1,0:T(8,128)}, u32[]{:S(2)}) copy-start(f32[64,64]{1,0:T(8,128)} %env.1) | copy-start | bytes 49156
  0.7 10.0 %copy-start.3 = (f32[64,128]{1,0:T(8,128)S(1)}, f32[64,128]{1,0:T(8,128)}, u32[]{:S(2)}) copy-start(f32[64,128]{1,0:T(8,128)} %mix.1) | copy-start | bytes 98308
  2.5 4.2 %copy-start.11 = (f32[4,128]{1,0:T(4,128)S(1)}, f32[4,128]{1,0:T(4,128)}, u32[]{:S(2)}) copy-start(f32[4,128]{1,0:T(4,128)} %get-tuple-element.31) | copy-start | bytes 6148
  2.5 12.6 %collective-permute-start = (f32[320,128]{1,0:T(8,128)}, f32[320,128]{1,0:T(8,128)S(1)}, u32[]{:S(2)}, u32[]{:S(2)}) collective-permute-start(f32[320,128]{1,0:T(8,128)} %get-tuple-element.27.pack), channel_id=1, source_target_pairs={{0,1},{1,0},{2,3},{3,2},{4,5},{5,4},{6,7},{7,6},{8,9},{9,8},{10,11... | collective-permute-start | bytes 491528 | tf_op jit(solution)/shard_map/ppermute | solution.py:30
  3.0 5.7 %copy-start.10 = (f32[4,128]{1,0:T(4,128)S(1)}, f32[4,128]{1,0:T(4,128)}, u32[]{:S(2)}) copy-start(f32[4,128]{1,0:T(4,128)} %get-tuple-element.32) | copy-start | bytes 6148
  3.0 12.1 %collective-permute-start.4 = (f32[8,128]{1,0:T(8,128)}, f32[8,128]{1,0:T(8,128)S(1)}, u32[]{:S(2)}, u32[]{:S(2)}) collective-permute-start(f32[8,128]{1,0:T(8,128)} %get-tuple-element.34), channel_id=1, source_target_pairs={{0,8},{1,9},{2,10},{3,11},{4,12},{5,13},{6,14},{7,15},{8,0},{9,1},... | collective-permute-start | bytes 12296 | tf_op jit(solution)/shard_map/ppermute | solution.py:30
  6.6 2.1 %copy-start.9 = (f32[4,128]{1,0:T(4,128)S(1)}, f32[4,128]{1,0:T(4,128)}, u32[]{:S(2)}) copy-start(f32[4,128]{1,0:T(4,128)} %get-tuple-element.33) | copy-start | bytes 6148
  6.7 6.0 %collective-permute-start.1 = (f32[4,128]{1,0:T(4,128)S(1)}, f32[4,128]{1,0:T(4,128)S(1)}, u32[]{:S(2)}, u32[]{:S(2)}) collective-permute-start(f32[4,128]{1,0:T(4,128)S(1)} %copy-done.11), channel_id=1, source_target_pairs={{0,15},{1,2},{2,1},{3,4},{4,3},{5,6},{6,5},{7,8},{8,7},{9,10},{10,... | collective-permute-start | bytes 6152 | tf_op jit(solution)/shard_map/ppermute | solution.py:30
  8.7 3.9 %collective-permute-start.2 = (f32[4,128]{1,0:T(4,128)S(1)}, f32[4,128]{1,0:T(4,128)S(1)}, u32[]{:S(2)}, u32[]{:S(2)}) collective-permute-start(f32[4,128]{1,0:T(4,128)S(1)} %copy-done.10), channel_id=1, source_target_pairs={{0,2},{1,3},{2,0},{3,1},{4,6},{5,7},{6,4},{7,5},{8,10},{9,11},{10,... | collective-permute-start | bytes 6152 | tf_op jit(solution)/shard_map/ppermute | solution.py:30
  8.7 1.9 %copy-start.6 = (f32[64,8]{0,1:T(8,128)S(1)}, f32[64,8]{0,1:T(8,128)}, u32[]{:S(2)}) copy-start(f32[64,8]{0,1:T(8,128)} %param.23) | copy-start | bytes 6148
  8.7 1.9 %copy-start.5 = (f32[64,8]{0,1:T(8,128)S(1)}, f32[64,8]{0,1:T(8,128)}, u32[]{:S(2)}) copy-start(f32[64,8]{0,1:T(8,128)} %param.21) | copy-start | bytes 6148
  8.7 6.3 %collective-permute-start.3 = (f32[4,128]{1,0:T(4,128)S(1)}, f32[4,128]{1,0:T(4,128)S(1)}, u32[]{:S(2)}, u32[]{:S(2)}) collective-permute-start(f32[4,128]{1,0:T(4,128)S(1)} %copy-done.9), channel_id=1, source_target_pairs={{0,14},{1,15},{2,4},{3,5},{4,2},{5,3},{6,8},{7,9},{8,6},{9,7},{10,... | collective-permute-start | bytes 6152 | tf_op jit(solution)/shard_map/ppermute | solution.py:30
  10.6 0.7 %copy-start.7 = (f32[64]{0:T(128)S(1)}, f32[64]{0:T(128)}, u32[]{:S(2)}) copy-start(f32[64]{0:T(128)} %param.22) | copy-start | bytes 772
  10.6 0.7 %copy-start.8 = (f32[64]{0:T(128)S(1)}, f32[64]{0:T(128)}, u32[]{:S(2)}) copy-start(f32[64]{0:T(128)} %param.27) | copy-start | bytes 772
  11.3 0.9 %copy-start = (f32[320,128]{1,0:T(8,128)S(1)}, f32[320,128]{1,0:T(8,128)}, u32[]{:S(2)}) copy-start(f32[320,128]{1,0:T(8,128)} %get-tuple-element.27.pack) | copy-start | bytes 491524
  39.6 8.5 %collective-permute-start.5 = (f32[32,128]{1,0:T(8,128)S(1)}, f32[32,128]{1,0:T(8,128)S(1)}, u32[]{:S(2)}, u32[]{:S(2)}) collective-permute-start(f32[32,128]{1,0:T(8,128)S(1)} %get-tuple-element.44), channel_id=1, source_target_pairs={{0,1},{1,0},{2,3},{3,2},{4,5},{5,4},{6,7},{7,6},{8,9},{9,8},{10,11... | collective-permute-start | bytes 49160 | tf_op jit(solution)/shard_map/ppermute | solution.py:30
  39.7 8.4 %copy-start.4 = (s32[6,128]{1,0:T(8,128)S(1)}, s32[6,128]{1,0:T(8,128)}, u32[]{:S(2)}) copy-start(s32[6,128]{1,0:T(8,128)} %ghost_index.3) | copy-start | bytes 9220
  39.7 8.4 %collective-permute-start.9 = (f32[8,128]{1,0:T(8,128)S(1)}, f32[8,128]{1,0:T(8,128)S(1)}, u32[]{:S(2)}, u32[]{:S(2)}) collective-permute-start(f32[8,128]{1,0:T(8,128)S(1)} %get-tuple-element.48), channel_id=1, source_target_pairs={{0,8},{1,9},{2,10},{3,11},{4,12},{5,13},{6,14},{7,15},{8,0},{9,1},... | collective-permute-start | bytes 12296 | tf_op jit(solution)/shard_map/ppermute | solution.py:30
  39.8 5.8 %collective-permute-start.6 = (f32[4,128]{1,0:T(4,128)S(1)}, f32[4,128]{1,0:T(4,128)S(1)}, u32[]{:S(2)}, u32[]{:S(2)}) collective-permute-start(f32[4,128]{1,0:T(4,128)S(1)} %get-tuple-element.45), channel_id=1, source_target_pairs={{0,15},{1,2},{2,1},{3,4},{4,3},{5,6},{6,5},{7,8},{8,7},{9,10},{10,... | collective-permute-start | bytes 6152 | tf_op jit(solution)/shard_map/ppermute | solution.py:30
  39.8 5.7 %collective-permute-start.7 = (f32[4,128]{1,0:T(4,128)S(1)}, f32[4,128]{1,0:T(4,128)S(1)}, u32[]{:S(2)}, u32[]{:S(2)}) collective-permute-start(f32[4,128]{1,0:T(4,128)S(1)} %get-tuple-element.46), channel_id=1, source_target_pairs={{0,2},{1,3},{2,0},{3,1},{4,6},{5,7},{6,4},{7,5},{8,10},{9,11},{10,... | collective-permute-start | bytes 6152 | tf_op jit(solution)/shard_map/ppermute | solution.py:30
  41.8 6.3 %collective-permute-start.8 = (f32[4,128]{1,0:T(4,128)S(1)}, f32[4,128]{1,0:T(4,128)S(1)}, u32[]{:S(2)}, u32[]{:S(2)}) collective-permute-start(f32[4,128]{1,0:T(4,128)S(1)} %get-tuple-element.47), channel_id=1, source_target_pairs={{0,14},{1,15},{2,4},{3,5},{4,2},{5,3},{6,8},{7,9},{8,6},{9,7},{10,... | collective-permute-start | bytes 6152 | tf_op jit(solution)/shard_map/ppermute | solution.py:30

commit v2 on v1

--- a/solution.py
+++ b/solution.py
@@ -84,7 +84,9 @@
     raise ValueError(a)
 
 
-def prep_kernel(zeta_table, escale, live, pos, species, ghost_index, nbr, pack, *sends, steps):
+def prep_kernel(
+    zeta_table, escale, live, pos, species, ghost_index, nbr, nbr_row, out_row, pack, *sends, steps
+):
     kinds = species[...]
     zeta = scale = jnp.zeros(kinds.shape, F32)
     for k in range(zeta_table.shape[0]):
@@ -99,6 +101,9 @@
         pack[8 * t : 8 * t + 6, :] = jnp.concatenate(parts, axis=0)
         pack[8 * t + 6 : 8 * t + 7, :] = jnp.zeros((1, LANES), F32)
         pack[8 * t + 7 : 8 * t + 8, :] = scale[:, lane]
+    chan = nbr_row.shape[1]
+    pack[38:39, :chan] = nbr_row[...]
+    pack[38:39, chan : 2 * chan] = out_row[...]
     pack[8 * tiles :, :] = nbr[...].astype(F32)
     index = ghost_index[...]
     index = jnp.concatenate([index, index[:2]], axis=0)
@@ -126,15 +131,16 @@
                     ref[row + d : row + d + 1, :] = part
 
 
-def weights_kernel(pack, center_t, nbr_row, radial_t, latent, env, mix, out_row, *outs):
+def weights_kernel(pack, center_t, radial_t, latent, env, mix, *outs):
     pack_o, out_wide_o, out_row2_o = outs[:3]
     pack_o[...] = pack[...]
     chan = latent.shape[0]
     kinds_total = center_t.shape[0]
+    nbr_row, row = pack[38:39, :chan], pack[38:39, chan : 2 * chan]
     norm = NBR ** (-0.5)
     nb = radial_t.shape[0]
     first = jnp.concatenate(
-        [radial_t[...], nbr_row[...], jnp.zeros((LANES - nb - 1, chan), F32)], axis=0
+        [radial_t[...], nbr_row, jnp.zeros((LANES - nb - 1, chan), F32)], axis=0
     ).T
     centers = jnp.concatenate([center_t[...], jnp.zeros((LANES - kinds_total, chan), F32)], axis=0).T
     top, rest = halves(0.5 * centers[:, :8])
@@ -142,7 +148,6 @@
     w2 = wide(0.5 * latent[...])
     mix_a = mix[:, :chan]
     mix_b = mix[:, chan:]
-    row = out_row[...]
     w3 = wide(jnp.concatenate([0.5 * mix_a, row, jnp.zeros((15, chan), F32)], axis=0))
     both = (0.5 * norm) * mm(wide(mix_b), stack(env[...]))
     out_col = jnp.broadcast_to(row, (LANES, chan)).T
@@ -233,8 +238,7 @@
                 table[0, tile, d : d + 1, :] = row
     acc_s[...] = jnp.zeros(acc_s.shape, F32)
     own_s[...] = jnp.zeros(own_s.shape, F32)
-    for ref in (keep_s, index_s, red_s, outf_s, db_s):
-        ref[...] = jnp.zeros(ref.shape, F32)
+    keep_s[...] = jnp.zeros(keep_s.shape, F32)
 
     w1, w2, w3, w4, w5, w6, w7, w8 = [ref[...] for ref in weights]
     out_row2 = row2[...]
@@ -335,7 +339,8 @@
             hit = sub16 == highs
             rows = [jnp.where(hit, force_s[q, n : n + 1, :], 0.0) for q in range(6)]
             lefts.append(jnp.concatenate(rows, axis=0).astype(BF16))
-        acc_s[which] += mm_nt(jnp.concatenate(lefts, axis=1), jnp.concatenate(rights, axis=1))
+        for c in range(0, NBR, 8):
+            acc_s[which] += mm_nt(jnp.concatenate(lefts[c : c + 8], axis=1), jnp.concatenate(rights[c : c + 8], axis=1))
 
     def block(i, carry):
         finish(*carry)
@@ -422,12 +427,12 @@
 
         def centre_sum(both_parts, t):
             found = mm_nt(ub_s[t], both_parts)
-            return found[:NBR] + jnp.where(lower, found[NBR:], 0.0)
+            return found[:24] + jnp.where(lower[:24], found[24:], 0.0)
 
         def spread_rows(sums, weight):
             top, rest = halves(jnp.concatenate(sums, axis=0))
             out = mm(jnp.concatenate([top, rest, top], axis=1), weight)
-            return [out[NBR * i : NBR * i + NBR] for i in range(len(sums))]
+            return [out[24 * i : 24 * i + 24] for i in range(len(sums))]
 
         def pieces(q, r):
             return [geo_s[q + d, r : r + 1, :] * masks[r % 2] for d in range(3)]
@@ -454,7 +459,7 @@
                     ua = jnp.concatenate([*a, *b, *a, zero8], axis=0)
                     ua_s[t, :, cell] = ua.astype(BF16)
                     a, b = pieces(6, r), pieces(9, r)
-                    ub = jnp.concatenate([*a, zero8, *b, zero8], axis=0)
+                    ub = jnp.concatenate([*a, *b], axis=0)
                     ub_s[t, :, cell] = ub.astype(BF16)
 
         def stage_first(ts):
@@ -478,7 +483,7 @@
         def stage_env(ts):
             for t, g in zip(ts, spread_rows([sums[t] for t in ts], w4)):
                 lefts[t] = terms(*parted(g))
-                top, rest = halves(g * out_row2)
+                top, rest = halves(jnp.concatenate([g * out_row2, zero8], axis=0))
                 rest = jnp.where(lower, rest, 0.0)[:, :80]
                 lefts[t, 1] = jnp.concatenate([w5, jnp.concatenate([top, rest], axis=1)], axis=0)
 
@@ -525,7 +530,7 @@
                 pulled = mm(lefts[t, 1], f2_s[t])
                 for r, h, cell in cells(t):
                     for d in range(3):
-                        part = pulled[8 * d : 8 * d + 8, cell] + pulled[NBR + 8 * d : NBR + 8 * d + 8, cell]
+                        part = pulled[8 * d : 8 * d + 8, cell] + pulled[24 + 8 * d : 32 + 8 * d, cell]
                         red_s[3 + d, 8 * r : 8 * r + 8, :] = part * masks[h]
 
         def stage_slope1(ts):
@@ -654,10 +659,20 @@
     pack, *sends = pl.pallas_call(
         functools.partial(prep_kernel, steps=steps),
         out_shape=[shape((8 * tiles + nbr.shape[0], LANES), F32)] + buffers,
-        in_specs=[SM(), SM(), SM()] + [VM()] * 4,
+        in_specs=[SM(), SM(), SM()] + [VM()] * 6,
         out_specs=[VM()] * (1 + len(buffers)),
         name="prep",
-    )(zeta_table, energy_scale, live_bins, positions, species.reshape(1, atoms), ghost_index, nbr)
+    )(
+        zeta_table,
+        energy_scale,
+        live_bins,
+        positions,
+        species.reshape(1, atoms),
+        ghost_index,
+        nbr,
+        nbr_embed.reshape(1, chan),
+        out_weight.reshape(1, chan),
+    )
     mate, *arrived = exchange([pack, *sends])
 
     heights = [(chan, 64), (chan, 3 * chan), (chan + 16, 3 * chan), (6 * chan, LANES)]
@@ -666,19 +681,17 @@
         weights_kernel,
         out_shape=[shape(pack.shape, F32), shape((chan, 2 * LANES), F32), shape((1, 2 * chan), F32)]
         + [shape(h, BF16) for h in heights],
-        in_specs=[VM()] * 8,
+        in_specs=[VM()] * 6,
         out_specs=[VM()] * (3 + len(heights)),
         compiler_params=SMALL,
         name="weights",
     )(
         pack,
         center_embed.T,
-        nbr_embed.reshape(1, chan),
         radial_weight.T,
         latent_weight,
         env_weight,
         mix_weight,
-        out_weight.reshape(1, chan),
     )
 
     pairs = NBR // 2
@@ -706,7 +719,7 @@
             big,
             pltpu.VMEM((pairs, 2 * chan, 2 * LANES), BF16),
             pltpu.VMEM((pairs, 80, 2 * LANES), BF16),
-            pltpu.VMEM((pairs, 2 * NBR, 2 * LANES), BF16),
+            pltpu.VMEM((pairs, 48, 2 * LANES), BF16),
             pltpu.VMEM((LANES, LANES), BF16),
         ],
         compiler_params=pltpu.CompilerParams(vmem_limit_bytes=24 * 1024 * 1024),

time: 49 us -> 49.9 us (1.018)
  the two profiles are of different devices: /device:TPU:0 before, /device:TPU:2 now
where the time goes in v2:
time: 49.9 us; the launch traced here: 50.7 us
  starting transfers between devices  22.6 us (45%)
  Pallas kernels  19.4 us (39%)
  waiting for transfers between devices  6.96 us (14%)
  local copies, waits for them, and re-layouts  0.94 us (2%)
  between operations  0.77 us (2%)
    ppermute x10, starting transfers between devices, swap(): return lax.ppermute(block, 'dom', [(i, partner(i)) for i in range(size)])  22.6 us
    pallas_call x1, Pallas kernels, shards(): pl.pallas_call(functools.partial(edge_kernel, steps=steps, batch=8, lag=1...  16.4 us
    ppermute x10, waiting for transfers between devices, swap(): return lax.ppermute(block, 'dom', [(i, partner(i)) for i in range(size)])  6.96 us
    pallas_call x1, Pallas kernels, shards(): pl.pallas_call(functools.partial(prep_kernel, steps=steps), out_shape=[sh...  1.74 us
  transfers between devices with their start and end apart: 10, of which 3 were waited for; matrix products, arithmetic and copies ran while one was open for 0% of the time, Pallas kernels for 1%

profile of v2, /device:TPU:2, one launch (start us, length us, event | category | flops | bytes accessed | tf_op | source)
XLA Modules:
  0.0 50.7 jit_solution(440297071450543517)
XLA Ops:
  0.7 0.0 copy-start.1
  0.7 0.0 copy-start.2
  0.7 0.0 copy-start.3
  0.7 1.7 %prep.1 = (f32[320,128]{1,0:T(8,128)}, f32[4,128]{1,0:T(4,128)}, f32[4,128]{1,0:T(4,128)}, f32[4,128]{1,0:T(4,128)}, f32[8,128]{1,0:T(8,128)}) custom-call(f32[8]{0:T(128)} %zeta_table.1, f32[8]{0:T(128)} %escale.1, s32[1]{0:T(128)S(6)} %copy.15.live, f32[3,1024]{1,0:T(4,128)} %pos.1, s32[1,1024]{1,0:T(1,128)} %bitcast.9, s32[6,128]{1,0:T(8,128)} %ghost_index.3, ...), custom_call_target="tpu_custom_call" | custom-call | tf_op jit(solution)/shard_map/prep/pallas_call | solution.py:659
  2.4 0.0 copy-start.8
  2.4 0.1 collective-permute-start
  2.5 0.0 copy-start.7
  2.5 2.7 %collective-permute-start.4 = (f32[8,128]{1,0:T(8,128)}, f32[8,128]{1,0:T(8,128)S(1)}, u32[]{:S(2)}, u32[]{:S(2)}) collective-permute-start(f32[8,128]{1,0:T(8,128)} %get-tuple-element.34), channel_id=1, source_target_pairs={{0,8},{1,9},{2,10},{3,11},{4,12},{5,13},{6,14},{7,15},{8,0},{9,1},... | collective-permute-start | bytes 12296 | tf_op jit(solution)/shard_map/ppermute | solution.py:30
  5.2 0.0 copy-start.6
  5.2 0.0 copy-start.5
  5.2 2.1 %collective-permute-start.1 = (f32[4,128]{1,0:T(4,128)}, f32[4,128]{1,0:T(4,128)S(1)}, u32[]{:S(2)}, u32[]{:S(2)}) collective-permute-start(f32[4,128]{1,0:T(4,128)} %get-tuple-element.31), channel_id=1, source_target_pairs={{0,15},{1,2},{2,1},{3,4},{4,3},{5,6},{6,5},{7,8},{8,7},{9,10},{10,... | collective-permute-start | bytes 6152 | tf_op jit(solution)/shard_map/ppermute | solution.py:30
  7.2 0.0 copy-done.8
  7.3 0.0 collective-permute-start.2
  7.3 0.0 copy-done.7
  7.3 1.9 %collective-permute-start.3 = (f32[4,128]{1,0:T(4,128)S(1)}, f32[4,128]{1,0:T(4,128)S(1)}, u32[]{:S(2)}, u32[]{:S(2)}) collective-permute-start(f32[4,128]{1,0:T(4,128)S(1)} %copy-done.7), channel_id=1, source_target_pairs={{0,14},{1,15},{2,4},{3,5},{4,2},{5,3},{6,8},{7,9},{8,6},{9,7},{10,... | collective-permute-start | bytes 6152 | tf_op jit(solution)/shard_map/ppermute | solution.py:30
  9.2 0.0 copy-done.1
  9.2 0.0 copy-done.2
  9.2 0.0 copy-done.3
  9.2 0.0 copy-done.6
  9.2 0.0 copy-done.5
  9.2 0.0 copy-start
  9.2 0.9 %copy-done = f32[320,128]{1,0:T(8,128)S(1)} copy-done((f32[320,128]{1,0:T(8,128)S(1)}, f32[320,128]{1,0:T(8,128)}, u32[]{:S(2)}) %copy-start) | copy-done | bytes 163864
  10.1 0.5 weights.1
  10.6 0.5 %collective-permute-done.1.refs_0_ = f32[4,128]{1,0:T(4,128)S(1)} collective-permute-done((f32[4,128]{1,0:T(4,128)}, f32[4,128]{1,0:T(4,128)S(1)}, u32[]{:S(2)}, u32[]{:S(2)}) %collective-permute-start.1) | collective-permute-done | bytes 2080 | tf_op jit(solution)/shard_map/ppermute | solution.py:30
  11.1 0.0 collective-permute-done.2.refs_1_
  11.1 2.5 %collective-permute-done.3.refs_2_ = f32[4,128]{1,0:T(4,128)S(1)} collective-permute-done((f32[4,128]{1,0:T(4,128)S(1)}, f32[4,128]{1,0:T(4,128)S(1)}, u32[]{:S(2)}, u32[]{:S(2)}) %collective-permute-start.3) | collective-permute-done | bytes 2080 | tf_op jit(solution)/shard_map/ppermute | solution.py:30
  13.6 0.0 collective-permute-done.4.refs_3_
  13.6 0.0 collective-permute-done.mate
  13.6 16.4 %edges.1 = (f32[3,1024]{1,0:T(4,128)S(1)}, f32[32,128]{1,0:T(8,128)S(1)}, f32[4,128]{1,0:T(4,128)S(1)}, f32[4,128]{1,0:T(4,128)S(1)}, f32[4,128]{1,0:T(4,128)S(1)}, /*index=5*/f32[8,128]{1,0:T(8,128)S(1)}) custom-call(s32[1]{0:T(128)S(6)} %copy.15.live, f32[320,128]{1,0:T(8,128)S(1)} %get-tuple-element.28.pack, f32[320,128]{1,0:T(8,128)S(1)} %collective-permute-done.mate, ...), custom_call_target="tpu_custom_call" | custom-call | tf_op jit(solution)/shard_map/edges/pallas_call | solution.py:699
  30.0 0.1 collective-permute-start.5
  30.1 0.0 copy-start.4
  30.1 0.1 collective-permute-start.9
  30.2 10.1 %collective-permute-start.6 = (f32[4,128]{1,0:T(4,128)S(1)}, f32[4,128]{1,0:T(4,128)S(1)}, u32[]{:S(2)}, u32[]{:S(2)}) collective-permute-start(f32[4,128]{1,0:T(4,128)S(1)} %get-tuple-element.45), channel_id=1, source_target_pairs={{0,15},{1,2},{2,1},{3,4},{4,3},{5,6},{6,5},{7,8},{8,7},{9,10},{10,... | collective-permute-start | bytes 6152 | tf_op jit(solution)/shard_map/ppermute | solution.py:30
  40.3 3.3 %collective-permute-start.7 = (f32[4,128]{1,0:T(4,128)S(1)}, f32[4,128]{1,0:T(4,128)S(1)}, u32[]{:S(2)}, u32[]{:S(2)}) collective-permute-start(f32[4,128]{1,0:T(4,128)S(1)} %get-tuple-element.46), channel_id=1, source_target_pairs={{0,2},{1,3},{2,0},{3,1},{4,6},{5,7},{6,4},{7,5},{8,10},{9,11},{10,... | collective-permute-start | bytes 6152 | tf_op jit(solution)/shard_map/ppermute | solution.py:30
  43.6 2.4 %collective-permute-start.8 = (f32[4,128]{1,0:T(4,128)S(1)}, f32[4,128]{1,0:T(4,128)S(1)}, u32[]{:S(2)}, u32[]{:S(2)}) collective-permute-start(f32[4,128]{1,0:T(4,128)S(1)} %get-tuple-element.47), channel_id=1, source_target_pairs={{0,14},{1,15},{2,4},{3,5},{4,2},{5,3},{6,8},{7,9},{8,6},{9,7},{10,... | collective-permute-start | bytes 6152 | tf_op jit(solution)/shard_map/ppermute | solution.py:30
  46.0 0.0 collective-permute-done.6.refs_0_
  46.0 0.0 collective-permute-done.7.refs_1_
  46.0 3.9 %collective-permute-done.8.refs_2_ = f32[4,128]{1,0:T(4,128)S(1)} collective-permute-done((f32[4,128]{1,0:T(4,128)S(1)}, f32[4,128]{1,0:T(4,128)S(1)}, u32[]{:S(2)}, u32[]{:S(2)}) %collective-permute-start.8) | collective-permute-done | bytes 2080 | tf_op jit(solution)/shard_map/ppermute | solution.py:30
  49.9 0.0 collective-permute-done.9.refs_3_
  49.9 0.0 collective-permute-done.5.back
  49.9 0.0 copy-done.4
  49.9 0.8 %fold.1 = f32[3,1024]{1,0:T(4,128)} custom-call(f32[3,1024]{1,0:T(4,128)S(1)} %get-tuple-element.43.own, f32[32,128]{1,0:T(8,128)S(1)} %collective-permute-done.5.back, s32[6,128]{1,0:T(8,128)S(1)} %copy-done.4, f32[4,128]{1,0:T(4,128)S(1)} %collective-permute-done.6.refs_0_, f32[4,128]{1,0:T(4,128)S(1)} %collective-permute-done.7.refs_1_, ...), custom_call_target="tpu_custom_call" | custom-call | tf_op jit(solution)/shard_map/fold/pallas_call | solution.py:729
Async XLA Ops:
  0.7 8.5 %copy-start.1 = (f32[64,64]{1,0:T(8,128)S(1)}, f32[64,64]{1,0:T(8,128)}, u32[]{:S(2)}) copy-start(f32[64,64]{1,0:T(8,128)} %latent.1) | copy-start | bytes 49156
  0.7 8.5 %copy-start.2 = (f32[64,64]{1,0:T(8,128)S(1)}, f32[64,64]{1,0:T(8,128)}, u32[]{:S(2)}) copy-start(f32[64,64]{1,0:T(8,128)} %env.1) | copy-start | bytes 49156
  0.7 8.5 %copy-start.3 = (f32[64,128]{1,0:T(8,128)S(1)}, f32[64,128]{1,0:T(8,128)}, u32[]{:S(2)}) copy-start(f32[64,128]{1,0:T(8,128)} %mix.1) | copy-start | bytes 98308
  2.4 4.8 %copy-start.8 = (f32[4,128]{1,0:T(4,128)S(1)}, f32[4,128]{1,0:T(4,128)}, u32[]{:S(2)}) copy-start(f32[4,128]{1,0:T(4,128)} %get-tuple-element.32) | copy-start | bytes 6148
  2.4 11.2 %collective-permute-start = (f32[320,128]{1,0:T(8,128)}, f32[320,128]{1,0:T(8,128)S(1)}, u32[]{:S(2)}, u32[]{:S(2)}) collective-permute-start(f32[320,128]{1,0:T(8,128)} %get-tuple-element.27.pack), channel_id=1, source_target_pairs={{0,1},{1,0},{2,3},{3,2},{4,5},{5,4},{6,7},{7,6},{8,9},{9,8},{10,11... | collective-permute-start | bytes 491528 | tf_op jit(solution)/shard_map/ppermute | solution.py:30
  2.5 4.7 %copy-start.7 = (f32[4,128]{1,0:T(4,128)S(1)}, f32[4,128]{1,0:T(4,128)}, u32[]{:S(2)}) copy-start(f32[4,128]{1,0:T(4,128)} %get-tuple-element.33) | copy-start | bytes 6148
  2.5 11.1 %collective-permute-start.4 = (f32[8,128]{1,0:T(8,128)}, f32[8,128]{1,0:T(8,128)S(1)}, u32[]{:S(2)}, u32[]{:S(2)}) collective-permute-start(f32[8,128]{1,0:T(8,128)} %get-tuple-element.34), channel_id=1, source_target_pairs={{0,8},{1,9},{2,10},{3,11},{4,12},{5,13},{6,14},{7,15},{8,0},{9,1},... | collective-permute-start | bytes 12296 | tf_op jit(solution)/shard_map/ppermute | solution.py:30
  5.2 4.0 %copy-start.6 = (f32[64,8]{0,1:T(8,128)S(1)}, f32[64,8]{0,1:T(8,128)}, u32[]{:S(2)}) copy-start(f32[64,8]{0,1:T(8,128)} %param.23) | copy-start | bytes 6148
  5.2 4.0 %copy-start.5 = (f32[64,8]{0,1:T(8,128)S(1)}, f32[64,8]{0,1:T(8,128)}, u32[]{:S(2)}) copy-start(f32[64,8]{0,1:T(8,128)} %param.21) | copy-start | bytes 6148
  5.2 5.9 %collective-permute-start.1 = (f32[4,128]{1,0:T(4,128)}, f32[4,128]{1,0:T(4,128)S(1)}, u32[]{:S(2)}, u32[]{:S(2)}) collective-permute-start(f32[4,128]{1,0:T(4,128)} %get-tuple-element.31), channel_id=1, source_target_pairs={{0,15},{1,2},{2,1},{3,4},{4,3},{5,6},{6,5},{7,8},{8,7},{9,10},{10,... | collective-permute-start | bytes 6152 | tf_op jit(solution)/shard_map/ppermute | solution.py:30
  7.3 3.8 %collective-permute-start.2 = (f32[4,128]{1,0:T(4,128)S(1)}, f32[4,128]{1,0:T(4,128)S(1)}, u32[]{:S(2)}, u32[]{:S(2)}) collective-permute-start(f32[4,128]{1,0:T(4,128)S(1)} %copy-done.8), channel_id=1, source_target_pairs={{0,2},{1,3},{2,0},{3,1},{4,6},{5,7},{6,4},{7,5},{8,10},{9,11},{10,... | collective-permute-start | bytes 6152 | tf_op jit(solution)/shard_map/ppermute | solution.py:30
  7.3 6.3 %collective-permute-start.3 = (f32[4,128]{1,0:T(4,128)S(1)}, f32[4,128]{1,0:T(4,128)S(1)}, u32[]{:S(2)}, u32[]{:S(2)}) collective-permute-start(f32[4,128]{1,0:T(4,128)S(1)} %copy-done.7), channel_id=1, source_target_pairs={{0,14},{1,15},{2,4},{3,5},{4,2},{5,3},{6,8},{7,9},{8,6},{9,7},{10,... | collective-permute-start | bytes 6152 | tf_op jit(solution)/shard_map/ppermute | solution.py:30
  9.2 0.9 %copy-start = (f32[320,128]{1,0:T(8,128)S(1)}, f32[320,128]{1,0:T(8,128)}, u32[]{:S(2)}) copy-start(f32[320,128]{1,0:T(8,128)} %get-tuple-element.27.pack) | copy-start | bytes 491524
  30.0 19.9 %collective-permute-start.5 = (f32[32,128]{1,0:T(8,128)S(1)}, f32[32,128]{1,0:T(8,128)S(1)}, u32[]{:S(2)}, u32[]{:S(2)}) collective-permute-start(f32[32,128]{1,0:T(8,128)S(1)} %get-tuple-element.44), channel_id=1, source_target_pairs={{0,1},{1,0},{2,3},{3,2},{4,5},{5,4},{6,7},{7,6},{8,9},{9,8},{10,11... | collective-permute-start | bytes 49160 | tf_op jit(solution)/shard_map/ppermute | solution.py:30
  30.1 19.8 %copy-start.4 = (s32[6,128]{1,0:T(8,128)S(1)}, s32[6,128]{1,0:T(8,128)}, u32[]{:S(2)}) copy-start(s32[6,128]{1,0:T(8,128)} %ghost_index.3) | copy-start | bytes 9220
  30.1 19.8 %collective-permute-start.9 = (f32[8,128]{1,0:T(8,128)S(1)}, f32[8,128]{1,0:T(8,128)S(1)}, u32[]{:S(2)}, u32[]{:S(2)}) collective-permute-start(f32[8,128]{1,0:T(8,128)S(1)} %get-tuple-element.48), channel_id=1, source_target_pairs={{0,8},{1,9},{2,10},{3,11},{4,12},{5,13},{6,14},{7,15},{8,0},{9,1},... | collective-permute-start | bytes 12296 | tf_op jit(solution)/shard_map/ppermute | solution.py:30
  30.2 15.8 %collective-permute-start.6 = (f32[4,128]{1,0:T(4,128)S(1)}, f32[4,128]{1,0:T(4,128)S(1)}, u32[]{:S(2)}, u32[]{:S(2)}) collective-permute-start(f32[4,128]{1,0:T(4,128)S(1)} %get-tuple-element.45), channel_id=1, source_target_pairs={{0,15},{1,2},{2,1},{3,4},{4,3},{5,6},{6,5},{7,8},{8,7},{9,10},{10,... | collective-permute-start | bytes 6152 | tf_op jit(solution)/shard_map/ppermute | solution.py:30
  40.3 5.7 %collective-permute-start.7 = (f32[4,128]{1,0:T(4,128)S(1)}, f32[4,128]{1,0:T(4,128)S(1)}, u32[]{:S(2)}, u32[]{:S(2)}) collective-permute-start(f32[4,128]{1,0:T(4,128)S(1)} %get-tuple-element.46), channel_id=1, source_target_pairs={{0,2},{1,3},{2,0},{3,1},{4,6},{5,7},{6,4},{7,5},{8,10},{9,11},{10,... | collective-permute-start | bytes 6152 | tf_op jit(solution)/shard_map/ppermute | solution.py:30
  43.6 6.3 %collective-permute-start.8 = (f32[4,128]{1,0:T(4,128)S(1)}, f32[4,128]{1,0:T(4,128)S(1)}, u32[]{:S(2)}, u32[]{:S(2)}) collective-permute-start(f32[4,128]{1,0:T(4,128)S(1)} %get-tuple-element.47), channel_id=1, source_target_pairs={{0,14},{1,15},{2,4},{3,5},{4,2},{5,3},{6,8},{7,9},{8,6},{9,7},{10,... | collective-permute-start | bytes 6152 | tf_op jit(solution)/shard_map/ppermute | solution.py:30
